TPU v7x, 512 devices: a whole 4x8x8 slice. The times are simulated.
512 devices in a mesh: ctx: 8 (over x, y_hi), head: 32 (over z, y_lo), pool: 2 (over core).
Axes of the slice: x: 4, y: 8 (y_hi: 2, y_lo: 4; y = y_hi * 4 + y_lo), z: 8, core: 2. Of those that a mesh axis runs over, the one named last changes fastest.
Arguments:
- queries: bfloat16 [2, 1024, 64, 576], P('pool', 'ctx', 'head')
- new_latent: bfloat16 [2, 1024, 576], P('pool', 'ctx')
- cache_pool: bfloat16 [8, 32, 64, 576], P('ctx', 'pool'), may hold values from -6 to 6
- block_list: int32 [2, 8, 16], P('pool', 'ctx'), may hold values from 0 to 31, as said below
- cached_lengths: int32 [2], P('pool'), may hold values from 2730 to 8192
- w_uv: bfloat16 [64, 512, 128], P('head'), may hold values from -4 to 4
- w_o: bfloat16 [64, 128, 7168], P('head'), may hold values from -0.125 to 0.125
Outputs:
- mixed: bfloat16 [2, 1024, 7168], P('pool', 'ctx', 'head')
Inputs may be any that keep to these rules, and one draw needn't show every extreme that they name: For each ctx index c, block_list[:, c, :] holds every slot 0 to 31 exactly once.
All inputs are finite; a program needn't handle non-finite values.
Results may differ from a plain program's by a relative error of at most 0.015.
Values may be sent and summed in bfloat16 or wider, within the bound.
A program may use at most 64 MiB of HBM per device.

v0:
```python
import jax
import jax.numpy as jnp
from jax import lax
from jax.sharding import PartitionSpec as P

LAT = 512


score_scale = 192.0 ** (-0.5)
neg_big = -1e30


def from_behind(value, axis, steps):
    count = lax.axis_size(axis)
    pairs = [(source, (source + steps) % count) for source in range(count)]
    return lax.ppermute(value, axis, pairs)


def key_visible(key_rows, query_rows, per_device, hist_device, new_device, cached):
    device_of = key_rows // per_device
    local_row = key_rows % per_device
    history_pos = device_of * hist_device + local_row
    new_pos = device_of * new_device + local_row - hist_device
    return jnp.where(
        (local_row < hist_device)[None, :],
        (history_pos < cached)[None, :],
        new_pos[None, :] <= query_rows[:, None],
    )


def online_update(softmax_state, query_block, key_block, visible):
    running_max, denominator, numerator = softmax_state
    scores = (
        jnp.einsum("thd,kd->thk", query_block, key_block, preferred_element_type=jnp.float32)
        * score_scale
    )
    seen = visible[:, None, :]
    scores = jnp.where(seen, scores, neg_big)
    new_max = jnp.maximum(running_max, jnp.max(scores, axis=2))
    factor = jnp.exp(running_max - new_max)
    weights = jnp.where(seen, jnp.exp(scores - new_max[..., None]), 0.0)
    denominator = denominator * factor + jnp.sum(weights, axis=2)
    value_block = key_block[:, :LAT].astype(jnp.float32)
    numerator = numerator * factor[..., None] + jnp.einsum(
        "thk,kl->thl", weights, value_block, preferred_element_type=jnp.float32
    )
    return (new_max, denominator, numerator)


def body(queries, new_latent, cache_pool, block_list, cached_lengths, w_uv, w_o):
    pooled = lax.all_gather(cache_pool, "pool", axis=1, tiled=True)
    history = jnp.take(pooled[0], block_list[0, 0], axis=0)
    hist_device = history.shape[0] * history.shape[1]
    history = history.reshape(hist_device, history.shape[2])
    all_keys = jnp.concatenate([history, new_latent[0]], axis=0)
    new_device = new_latent.shape[1]
    per_device = all_keys.shape[0]
    cycle_size = lax.axis_size("ctx")
    cycle_index = lax.axis_index("ctx")
    cached = cached_lengths[0]
    query_block = queries[0]
    heads_here = query_block.shape[1]
    offsets = jnp.arange(new_device, dtype=jnp.int32)
    start_state = (
        jnp.full((new_device, heads_here), neg_big, jnp.float32),
        jnp.zeros((new_device, heads_here), jnp.float32),
        jnp.zeros((new_device, heads_here, LAT), jnp.float32),
    )
    local_rows = cycle_index * per_device + jnp.arange(per_device, dtype=jnp.int32)
    softmax_state = start_state
    for cycle_step in range(cycle_size):
        anchor = (cycle_index - cycle_step) % cycle_size
        query_rows = anchor * new_device + offsets
        visible = key_visible(local_rows, query_rows, per_device, hist_device, new_device, cached)
        softmax_state = online_update(softmax_state, query_block, all_keys, visible)
        if cycle_step + 1 < cycle_size:
            query_block = from_behind(query_block, "ctx", 1)
        softmax_state = from_behind(
            (softmax_state[0], softmax_state[1], softmax_state[2]), "ctx", 1
        )
    running_max, denominator, numerator = softmax_state
    latent_out = (numerator / denominator[..., None]).astype(jnp.bfloat16)
    head_out = jnp.einsum("thl,hlv->thv", latent_out, w_uv, preferred_element_type=jnp.float32)
    head_out = head_out.astype(jnp.bfloat16)
    partial_out = jnp.einsum("thv,hvd->td", head_out, w_o, preferred_element_type=jnp.float32)
    summed = lax.psum(partial_out, "head")
    col_width = partial_out.shape[1] // lax.axis_size("head")
    own_columns = lax.dynamic_slice_in_dim(summed, lax.axis_index("head") * col_width, col_width, 1)
    return own_columns.astype(jnp.bfloat16)[None]


def solution(mesh):
    in_specs = (
        P("pool", "ctx", "head", None),
        P("pool", "ctx", None),
        P("ctx", "pool", None, None),
        P("pool", "ctx", None),
        P("pool"),
        P("head", None, None),
        P("head", None, None),
    )
    out_specs = P("pool", "ctx", "head")
    return jax.shard_map(body, mesh=mesh, in_specs=in_specs, out_specs=out_specs, check_vma=False)
```

profile of v0, /device:TPU:6, one launch (start us, length us, event | category | flops | bytes accessed | tf_op | source)
XLA Modules:
  0.0 594.9 jit_solution(13551681991266776281)
XLA Ops:
  6.5 7.9 %collective-permute-start.2 = (bf16[128,2,576]{0,2,1:T(8,128)(2,1)}, bf16[128,2,576]{0,2,1:T(8,128)(2,1)S(1)}, u32[]{:S(2)}, u32[]{:S(2)}) collective-permute-start(bf16[128,2,576]{0,2,1:T(8,128)(2,1)} %bitcast.121), channel_id=1, source_target_pairs={{0,64},{64,128},{128,192},{192,256},{256,320},{320,384},{384,448},... | collective-permute-start | bytes 884744 | tf_op jit(solution)/shard_map/ppermute | solution.py:16
  14.4 12.7 %collective-permute-done.2 = bf16[128,2,576]{0,2,1:T(8,128)(2,1)S(1)} collective-permute-done((bf16[128,2,576]{0,2,1:T(8,128)(2,1)}, bf16[128,2,576]{0,2,1:T(8,128)(2,1)S(1)}, u32[]{:S(2)}, u32[]{:S(2)}) %collective-permute-start.2) | collective-permute-done | bytes 294944 | tf_op jit(solution)/shard_map/ppermute | solution.py:16
  27.2 8.2 %collective-permute-start.5 = (bf16[128,2,576]{0,2,1:T(8,128)(2,1)S(1)}, bf16[128,2,576]{0,2,1:T(8,128)(2,1)S(1)}, u32[]{:S(2)}, u32[]{:S(2)}) collective-permute-start(bf16[128,2,576]{0,2,1:T(8,128)(2,1)S(1)} %collective-permute-done.2), channel_id=1, source_target_pairs={{0,64},{64,128},{128,192},{192,256},{256,320},{320,384},{384,448},... | collective-permute-start | bytes 884744 | tf_op jit(solution)/shard_map/ppermute | solution.py:16
  36.2 11.5 %collective-permute-done.5 = bf16[128,2,576]{0,2,1:T(8,128)(2,1)S(1)} collective-permute-done((bf16[128,2,576]{0,2,1:T(8,128)(2,1)S(1)}, bf16[128,2,576]{0,2,1:T(8,128)(2,1)S(1)}, u32[]{:S(2)}, u32[]{:S(2)}) %collective-permute-start.5) | collective-permute-done | bytes 294944 | tf_op jit(solution)/shard_map/ppermute | solution.py:16
  47.7 8.3 %collective-permute-start.8 = (bf16[128,2,576]{0,2,1:T(8,128)(2,1)S(1)}, bf16[128,2,576]{0,2,1:T(8,128)(2,1)S(1)}, u32[]{:S(2)}, u32[]{:S(2)}) collective-permute-start(bf16[128,2,576]{0,2,1:T(8,128)(2,1)S(1)} %collective-permute-done.5), channel_id=1, source_target_pairs={{0,64},{64,128},{128,192},{192,256},{256,320},{320,384},{384,448},... | collective-permute-start | bytes 884744 | tf_op jit(solution)/shard_map/ppermute | solution.py:16
  56.1 14.2 %collective-permute-done.8 = bf16[128,2,576]{0,2,1:T(8,128)(2,1)S(1)} collective-permute-done((bf16[128,2,576]{0,2,1:T(8,128)(2,1)S(1)}, bf16[128,2,576]{0,2,1:T(8,128)(2,1)S(1)}, u32[]{:S(2)}, u32[]{:S(2)}) %collective-permute-start.8) | collective-permute-done | bytes 294944 | tf_op jit(solution)/shard_map/ppermute | solution.py:16
  70.3 4.2 collective-permute-start.11
  74.5 11.5 %collective-permute-done.11 = bf16[128,2,576]{0,2,1:T(8,128)(2,1)S(1)} collective-permute-done((bf16[128,2,576]{0,2,1:T(8,128)(2,1)S(1)}, bf16[128,2,576]{0,2,1:T(8,128)(2,1)S(1)}, u32[]{:S(2)}, u32[]{:S(2)}) %collective-permute-start.11) | collective-permute-done | bytes 294944 | tf_op jit(solution)/shard_map/ppermute | solution.py:16
  86.1 3.1 collective-permute-start.14
  89.2 2.2 compare_select_fusion
  91.5 10.0 %collective-permute-done.14 = bf16[128,2,576]{0,2,1:T(8,128)(2,1)S(1)} collective-permute-done((bf16[128,2,576]{0,2,1:T(8,128)(2,1)S(1)}, bf16[128,2,576]{0,2,1:T(8,128)(2,1)S(1)}, u32[]{:S(2)}, u32[]{:S(2)}) %collective-permute-start.14) | collective-permute-done | bytes 294944 | tf_op jit(solution)/shard_map/ppermute | solution.py:16
  101.5 4.2 collective-permute-start.17
  105.8 10.6 %collective-permute-done.17 = bf16[128,2,576]{0,2,1:T(8,128)(2,1)} collective-permute-done((bf16[128,2,576]{0,2,1:T(8,128)(2,1)S(1)}, bf16[128,2,576]{0,2,1:T(8,128)(2,1)}, u32[]{:S(2)}, u32[]{:S(2)}) %collective-permute-start.17) | collective-permute-done | bytes 294944 | tf_op jit(solution)/shard_map/ppermute | solution.py:16
  116.3 5.5 collective-permute-start.20
  121.9 2.5 gather_fusion
  127.7 7.0 %collective-permute-start.1 = (f32[128,2]{0,1:T(2,128)S(1)}, f32[128,2]{0,1:T(2,128)S(1)}, u32[]{:S(2)}, u32[]{:S(2)}) collective-permute-start(f32[128,2]{0,1:T(2,128)S(1)} %broadcast_maximum_fusion), channel_id=1, source_target_pairs={{0,64},{64,128},{128,192},{192,256},{256,320},{320,384},{384,448},... | collective-permute-start | bytes 3080 | tf_op jit(solution)/shard_map/ppermute | solution.py:16
  135.6 1.9 collective-permute-start
  137.5 5.4 collective-permute-start.22
  143.7 4.2 collective-permute-start.4
  148.1 11.9 %collective-permute-done.22 = f32[128,2]{0,1:T(2,128)S(1)} collective-permute-done((f32[128,2]{0,1:T(2,128)S(1)}, f32[128,2]{0,1:T(2,128)S(1)}, u32[]{:S(2)}, u32[]{:S(2)}) %collective-permute-start.22) | collective-permute-done | bytes 1056 | tf_op jit(solution)/shard_map/ppermute | solution.py:16
  160.6 4.3 collective-permute-start.3
  165.6 7.3 %collective-permute-start.23 = (f32[128,2]{0,1:T(2,128)S(1)}, f32[128,2]{0,1:T(2,128)S(1)}, u32[]{:S(2)}, u32[]{:S(2)}) collective-permute-start(f32[128,2]{0,1:T(2,128)S(1)} %get-tuple-element.17), channel_id=1, source_target_pairs={{0,64},{64,128},{128,192},{192,256},{256,320},{320,384},{384,448},... | collective-permute-start | bytes 3080 | tf_op jit(solution)/shard_map/ppermute | solution.py:16
  172.9 3.1 collective-permute-start.7
  176.2 9.5 %collective-permute-done.23 = f32[128,2]{0,1:T(2,128)S(1)} collective-permute-done((f32[128,2]{0,1:T(2,128)S(1)}, f32[128,2]{0,1:T(2,128)S(1)}, u32[]{:S(2)}, u32[]{:S(2)}) %collective-permute-start.23) | collective-permute-done | bytes 1056 | tf_op jit(solution)/shard_map/ppermute | solution.py:16
  186.3 3.9 collective-permute-start.6
  190.9 6.7 %collective-permute-start.24 = (f32[128,2]{0,1:T(2,128)S(1)}, f32[128,2]{0,1:T(2,128)S(1)}, u32[]{:S(2)}, u32[]{:S(2)}) collective-permute-start(f32[128,2]{0,1:T(2,128)S(1)} %get-tuple-element.15), channel_id=1, source_target_pairs={{0,64},{64,128},{128,192},{192,256},{256,320},{320,384},{384,448},... | collective-permute-start | bytes 3080 | tf_op jit(solution)/shard_map/ppermute | solution.py:16
  197.6 1.9 collective-permute-start.10
  199.8 10.0 %collective-permute-done.24 = f32[128,2]{0,1:T(2,128)S(1)} collective-permute-done((f32[128,2]{0,1:T(2,128)S(1)}, f32[128,2]{0,1:T(2,128)S(1)}, u32[]{:S(2)}, u32[]{:S(2)}) %collective-permute-start.24) | collective-permute-done | bytes 1056 | tf_op jit(solution)/shard_map/ppermute | solution.py:16
  210.4 4.4 collective-permute-start.9
  215.6 7.3 %collective-permute-start.25 = (f32[128,2]{0,1:T(2,128)S(1)}, f32[128,2]{0,1:T(2,128)S(1)}, u32[]{:S(2)}, u32[]{:S(2)}) collective-permute-start(f32[128,2]{0,1:T(2,128)S(1)} %get-tuple-element.13), channel_id=1, source_target_pairs={{0,64},{64,128},{128,192},{192,256},{256,320},{320,384},{384,448},... | collective-permute-start | bytes 3080 | tf_op jit(solution)/shard_map/ppermute | solution.py:16
  222.9 3.0 collective-permute-start.13
  226.2 9.5 %collective-permute-done.25 = f32[128,2]{0,1:T(2,128)S(1)} collective-permute-done((f32[128,2]{0,1:T(2,128)S(1)}, f32[128,2]{0,1:T(2,128)S(1)}, u32[]{:S(2)}, u32[]{:S(2)}) %collective-permute-start.25) | collective-permute-done | bytes 1056 | tf_op jit(solution)/shard_map/ppermute | solution.py:16
  236.2 3.9 collective-permute-start.12
  240.8 6.7 %collective-permute-start.26 = (f32[128,2]{0,1:T(2,128)S(1)}, f32[128,2]{0,1:T(2,128)S(1)}, u32[]{:S(2)}, u32[]{:S(2)}) collective-permute-start(f32[128,2]{0,1:T(2,128)S(1)} %get-tuple-element.11), channel_id=1, source_target_pairs={{0,64},{64,128},{128,192},{192,256},{256,320},{320,384},{384,448},... | collective-permute-start | bytes 3080 | tf_op jit(solution)/shard_map/ppermute | solution.py:16
  247.6 2.1 collective-permute-start.16
  249.9 9.8 %collective-permute-done.26 = f32[128,2]{0,1:T(2,128)S(1)} collective-permute-done((f32[128,2]{0,1:T(2,128)S(1)}, f32[128,2]{0,1:T(2,128)S(1)}, u32[]{:S(2)}, u32[]{:S(2)}) %collective-permute-start.26) | collective-permute-done | bytes 1056 | tf_op jit(solution)/shard_map/ppermute | solution.py:16
  260.3 4.4 collective-permute-start.15
  266.5 7.3 %collective-permute-start.27 = (f32[128,2]{0,1:T(2,128)S(1)}, f32[128,2]{0,1:T(2,128)S(1)}, u32[]{:S(2)}, u32[]{:S(2)}) collective-permute-start(f32[128,2]{0,1:T(2,128)S(1)} %get-tuple-element.9), channel_id=1, source_target_pairs={{0,64},{64,128},{128,192},{192,256},{256,320},{320,384},{384,448},... | collective-permute-start | bytes 3080 | tf_op jit(solution)/shard_map/ppermute | solution.py:16
  273.8 3.0 collective-permute-start.19
  277.1 8.5 %collective-permute-done.27 = f32[128,2]{0,1:T(2,128)S(1)} collective-permute-done((f32[128,2]{0,1:T(2,128)S(1)}, f32[128,2]{0,1:T(2,128)S(1)}, u32[]{:S(2)}, u32[]{:S(2)}) %collective-permute-start.27) | collective-permute-done | bytes 1056 | tf_op jit(solution)/shard_map/ppermute | solution.py:16
  286.2 3.9 collective-permute-start.18
  291.7 6.7 %collective-permute-start.28 = (f32[128,2]{0,1:T(2,128)S(1)}, f32[128,2]{0,1:T(2,128)S(1)}, u32[]{:S(2)}, u32[]{:S(2)}) collective-permute-start(f32[128,2]{0,1:T(2,128)S(1)} %get-tuple-element.7), channel_id=1, source_target_pairs={{0,64},{64,128},{128,192},{192,256},{256,320},{320,384},{384,448},... | collective-permute-start | bytes 3080 | tf_op jit(solution)/shard_map/ppermute | solution.py:16
  298.7 10.9 %collective-permute-done.28 = f32[128,2]{0,1:T(2,128)S(1)} collective-permute-done((f32[128,2]{0,1:T(2,128)S(1)}, f32[128,2]{0,1:T(2,128)S(1)}, u32[]{:S(2)}, u32[]{:S(2)}) %collective-permute-start.28) | collective-permute-done | bytes 1056 | tf_op jit(solution)/shard_map/ppermute | solution.py:16
  310.2 4.5 collective-permute-start.21
  314.7 7.3 %collective-permute-start.29 = (f32[128,2]{0,1:T(2,128)S(1)}, f32[128,2]{0,1:T(2,128)S(1)}, u32[]{:S(2)}, u32[]{:S(2)}) collective-permute-start(f32[128,2]{0,1:T(2,128)S(1)} %get-tuple-element.5), channel_id=1, source_target_pairs={{0,64},{64,128},{128,192},{192,256},{256,320},{320,384},{384,448},... | collective-permute-start | bytes 3080 | tf_op jit(solution)/shard_map/ppermute | solution.py:16
  322.0 7.6 %collective-permute-done.29 = f32[128,2]{0,1:T(2,128)S(1)} collective-permute-done((f32[128,2]{0,1:T(2,128)S(1)}, f32[128,2]{0,1:T(2,128)S(1)}, u32[]{:S(2)}, u32[]{:S(2)}) %collective-permute-start.29) | collective-permute-done | bytes 1056 | tf_op jit(solution)/shard_map/ppermute | solution.py:16
  329.6 5.5 convolution_bitcast_fusion
  335.1 252.4 %all-reduce.1 = bf16[128,7168]{0,1:T(8,128)(2,1)S(1)} all-reduce(f32[128,7168]{0,1:T(8,128)} %convolution_bitcast_fusion), channel_id=1, replica_groups=mesh['ctx'=8,'head'=32,'pool'=2] {'head'}, use_global_device_ids=true, to_apply=%region_16.17 | all-reduce | flops 917504 | bytes 5505024 | tf_op jit(solution)/shard_map/psum | solution.py:86
  (108 shorter events, 17.7 us)
Async XLA Ops:
  6.5 323.1 %copy-start = (bf16[2,512,128]{2,1,0:T(8,128)(2,1)S(1)}, bf16[2,512,128]{2,1,0:T(8,128)(2,1)}, u32[]{:S(2)}) copy-start(bf16[2,512,128]{2,1,0:T(8,128)(2,1)} %param.12) | copy-start | bytes 786436
  6.5 115.4 %all-gather.2.cloned.1.call-start = ((), (), s32[]{:S(2)}) async-start(), calls=%async_computation | async-start | bytes 3932160 | tf_op jit(solution)/shard_map/all_gather | solution.py:51
  6.5 20.6 %collective-permute-start.2 = (bf16[128,2,576]{0,2,1:T(8,128)(2,1)}, bf16[128,2,576]{0,2,1:T(8,128)(2,1)S(1)}, u32[]{:S(2)}, u32[]{:S(2)}) collective-permute-start(bf16[128,2,576]{0,2,1:T(8,128)(2,1)} %bitcast.121), channel_id=1, source_target_pairs={{0,64},{64,128},{128,192},{192,256},{256,320},{320,384},{384,448},... | collective-permute-start | bytes 884744 | tf_op jit(solution)/shard_map/ppermute | solution.py:16
  14.4 77.0 %copy-start.16 = (s32[1,1,16]{2,1,0:T(1,128)S(1)}, s32[1,1,16]{2,1,0:T(1,128)}, u32[]{:S(2)}) copy-start(s32[1,1,16]{2,1,0:T(1,128)} %param.10) | copy-start | bytes 196
  27.2 62.0 %copy-start.8 = (bf16[128,2,576]{0,2,1:T(8,128)(2,1)}, bf16[128,2,576]{0,2,1:T(8,128)(2,1)S(1)}, u32[]{:S(2)}) copy-start(bf16[128,2,576]{0,2,1:T(8,128)(2,1)S(1)} %collective-permute-done.2) | copy-start | bytes 884740
  27.2 20.5 %collective-permute-start.5 = (bf16[128,2,576]{0,2,1:T(8,128)(2,1)S(1)}, bf16[128,2,576]{0,2,1:T(8,128)(2,1)S(1)}, u32[]{:S(2)}, u32[]{:S(2)}) collective-permute-start(bf16[128,2,576]{0,2,1:T(8,128)(2,1)S(1)} %collective-permute-done.2), channel_id=1, source_target_pairs={{0,64},{64,128},{128,192},{192,256},{256,320},{320,384},{384,448},... | collective-permute-start | bytes 884744 | tf_op jit(solution)/shard_map/ppermute | solution.py:16
  47.7 41.5 %copy-start.6 = (bf16[128,2,576]{0,2,1:T(8,128)(2,1)}, bf16[128,2,576]{0,2,1:T(8,128)(2,1)S(1)}, u32[]{:S(2)}) copy-start(bf16[128,2,576]{0,2,1:T(8,128)(2,1)S(1)} %collective-permute-done.5) | copy-start | bytes 884740
  47.7 22.6 %collective-permute-start.8 = (bf16[128,2,576]{0,2,1:T(8,128)(2,1)S(1)}, bf16[128,2,576]{0,2,1:T(8,128)(2,1)S(1)}, u32[]{:S(2)}, u32[]{:S(2)}) collective-permute-start(bf16[128,2,576]{0,2,1:T(8,128)(2,1)S(1)} %collective-permute-done.5), channel_id=1, source_target_pairs={{0,64},{64,128},{128,192},{192,256},{256,320},{320,384},{384,448},... | collective-permute-start | bytes 884744 | tf_op jit(solution)/shard_map/ppermute | solution.py:16
  70.2 18.9 %copy-start.14 = (bf16[128,2,576]{0,2,1:T(8,128)(2,1)}, bf16[128,2,576]{0,2,1:T(8,128)(2,1)S(1)}, u32[]{:S(2)}) copy-start(bf16[128,2,576]{0,2,1:T(8,128)(2,1)S(1)} %collective-permute-done.8) | copy-start | bytes 884740
  70.3 15.8 %collective-permute-start.11 = (bf16[128,2,576]{0,2,1:T(8,128)(2,1)S(1)}, bf16[128,2,576]{0,2,1:T(8,128)(2,1)S(1)}, u32[]{:S(2)}, u32[]{:S(2)}) collective-permute-start(bf16[128,2,576]{0,2,1:T(8,128)(2,1)S(1)} %collective-permute-done.8), channel_id=1, source_target_pairs={{0,64},{64,128},{128,192},{192,256},{256,320},{320,384},{384,448},... | collective-permute-start | bytes 884744 | tf_op jit(solution)/shard_map/ppermute | solution.py:16
  86.1 38.4 %copy-start.12 = (bf16[128,2,576]{0,2,1:T(8,128)(2,1)}, bf16[128,2,576]{0,2,1:T(8,128)(2,1)S(1)}, u32[]{:S(2)}) copy-start(bf16[128,2,576]{0,2,1:T(8,128)(2,1)S(1)} %collective-permute-done.11) | copy-start | bytes 884740
  86.1 15.5 %collective-permute-start.14 = (bf16[128,2,576]{0,2,1:T(8,128)(2,1)S(1)}, bf16[128,2,576]{0,2,1:T(8,128)(2,1)S(1)}, u32[]{:S(2)}, u32[]{:S(2)}) collective-permute-start(bf16[128,2,576]{0,2,1:T(8,128)(2,1)S(1)} %collective-permute-done.11), channel_id=1, source_target_pairs={{0,64},{64,128},{128,192},{192,256},{256,320},{320,384},{384,448},... | collective-permute-start | bytes 884744 | tf_op jit(solution)/shard_map/ppermute | solution.py:16
  101.5 22.9 %copy-start.10 = (bf16[128,2,576]{0,2,1:T(8,128)(2,1)}, bf16[128,2,576]{0,2,1:T(8,128)(2,1)S(1)}, u32[]{:S(2)}) copy-start(bf16[128,2,576]{0,2,1:T(8,128)(2,1)S(1)} %collective-permute-done.14) | copy-start | bytes 884740
  101.5 14.8 %collective-permute-start.17 = (bf16[128,2,576]{0,2,1:T(8,128)(2,1)S(1)}, bf16[128,2,576]{0,2,1:T(8,128)(2,1)}, u32[]{:S(2)}, u32[]{:S(2)}) collective-permute-start(bf16[128,2,576]{0,2,1:T(8,128)(2,1)S(1)} %collective-permute-done.14), channel_id=1, source_target_pairs={{0,64},{64,128},{128,192},{192,256},{256,320},{320,384},{384,448},... | collective-permute-start | bytes 884744 | tf_op jit(solution)/shard_map/ppermute | solution.py:16
  116.3 173.7 %collective-permute-start.20 = (bf16[128,2,576]{0,2,1:T(8,128)(2,1)}, bf16[128,2,576]{0,2,1:T(8,128)(2,1)}, u32[]{:S(2)}, u32[]{:S(2)}) collective-permute-start(bf16[128,2,576]{0,2,1:T(8,128)(2,1)} %collective-permute-done.17), channel_id=1, source_target_pairs={{0,64},{64,128},{128,192},{192,256},{256,320},{320,384},{384,448},... | collective-permute-start | bytes 884744 | tf_op jit(solution)/shard_map/ppermute | solution.py:16
  125.1 0.9 copy-start.4
  126.0 0.9 copy-start.3
  126.0 1.0 copy-start.5
  127.7 15.9 %collective-permute-start.1 = (f32[128,2]{0,1:T(2,128)S(1)}, f32[128,2]{0,1:T(2,128)S(1)}, u32[]{:S(2)}, u32[]{:S(2)}) collective-permute-start(f32[128,2]{0,1:T(2,128)S(1)} %broadcast_maximum_fusion), channel_id=1, source_target_pairs={{0,64},{64,128},{128,192},{192,256},{256,320},{320,384},{384,448},... | collective-permute-start | bytes 3080 | tf_op jit(solution)/shard_map/ppermute | solution.py:16
  135.0 8.0 %copy-start.2 = (pred[128,1152]{0,1:T(8,128)(4,1)S(1)}, pred[128,1152]{0,1:T(8,128)(4,1)}, u32[]{:S(2)}) copy-start(pred[128,1152]{0,1:T(8,128)(4,1)} %get-tuple-element.20) | copy-start | bytes 442372
  135.0 8.0 %copy-start.9 = (bf16[128,2,576]{0,2,1:T(8,128)(2,1)S(1)}, bf16[128,2,576]{0,2,1:T(8,128)(2,1)}, u32[]{:S(2)}) copy-start(bf16[128,2,576]{0,2,1:T(8,128)(2,1)} %copy-done.8) | copy-start | bytes 884740
  135.6 24.4 %collective-permute-start = (f32[128,2,512]{2,0,1:T(8,128)S(1)}, f32[128,2,512]{2,0,1:T(8,128)S(1)}, u32[]{:S(2)}, u32[]{:S(2)}) collective-permute-start(f32[128,2,512]{2,0,1:T(8,128)S(1)} %convolution_add_fusion), channel_id=1, source_target_pairs={{0,64},{64,128},{128,192},{192,256},{256,320},{320,384},{384,448},... | collective-permute-start | bytes 1572872 | tf_op jit(solution)/shard_map/ppermute | solution.py:16
  137.5 22.4 %collective-permute-start.22 = (f32[128,2]{0,1:T(2,128)S(1)}, f32[128,2]{0,1:T(2,128)S(1)}, u32[]{:S(2)}, u32[]{:S(2)}) collective-permute-start(f32[128,2]{0,1:T(2,128)S(1)} %get-tuple-element.27), channel_id=1, source_target_pairs={{0,64},{64,128},{128,192},{192,256},{256,320},{320,384},{384,448},... | collective-permute-start | bytes 3080 | tf_op jit(solution)/shard_map/ppermute | solution.py:16
  143.7 29.2 %collective-permute-start.4 = (f32[128,2]{0,1:T(2,128)S(1)}, f32[128,2]{0,1:T(2,128)S(1)}, u32[]{:S(2)}, u32[]{:S(2)}) collective-permute-start(f32[128,2]{0,1:T(2,128)S(1)} %max.21), channel_id=1, source_target_pairs={{0,64},{64,128},{128,192},{192,256},{256,320},{320,384},{384,448},... | collective-permute-start | bytes 3080 | tf_op jit(solution)/shard_map/ppermute | solution.py:16
  160.0 4.9 copy-start.1
  160.0 4.9 copy-start.7
  160.6 25.2 %collective-permute-start.3 = (f32[128,2,512]{2,0,1:T(8,128)S(1)}, f32[128,2,512]{2,0,1:T(8,128)S(1)}, u32[]{:S(2)}, u32[]{:S(2)}) collective-permute-start(f32[128,2,512]{2,0,1:T(8,128)S(1)} %multiply_add_fusion.6), channel_id=1, source_target_pairs={{0,64},{64,128},{128,192},{192,256},{256,320},{320,384},{384,448},... | collective-permute-start | bytes 1572872 | tf_op jit(solution)/shard_map/ppermute | solution.py:16
  165.6 20.1 %collective-permute-start.23 = (f32[128,2]{0,1:T(2,128)S(1)}, f32[128,2]{0,1:T(2,128)S(1)}, u32[]{:S(2)}, u32[]{:S(2)}) collective-permute-start(f32[128,2]{0,1:T(2,128)S(1)} %get-tuple-element.17), channel_id=1, source_target_pairs={{0,64},{64,128},{128,192},{192,256},{256,320},{320,384},{384,448},... | collective-permute-start | bytes 3080 | tf_op jit(solution)/shard_map/ppermute | solution.py:16
  172.9 24.7 %collective-permute-start.7 = (f32[128,2]{0,1:T(2,128)S(1)}, f32[128,2]{0,1:T(2,128)S(1)}, u32[]{:S(2)}, u32[]{:S(2)}) collective-permute-start(f32[128,2]{0,1:T(2,128)S(1)} %max.22), channel_id=1, source_target_pairs={{0,64},{64,128},{128,192},{192,256},{256,320},{320,384},{384,448},... | collective-permute-start | bytes 3080 | tf_op jit(solution)/shard_map/ppermute | solution.py:16
  185.7 4.5 copy-start.15
  186.3 23.5 %collective-permute-start.6 = (f32[128,2,512]{2,0,1:T(8,128)S(1)}, f32[128,2,512]{2,0,1:T(8,128)S(1)}, u32[]{:S(2)}, u32[]{:S(2)}) collective-permute-start(f32[128,2,512]{2,0,1:T(8,128)S(1)} %multiply_add_fusion.5), channel_id=1, source_target_pairs={{0,64},{64,128},{128,192},{192,256},{256,320},{320,384},{384,448},... | collective-permute-start | bytes 1572872 | tf_op jit(solution)/shard_map/ppermute | solution.py:16
  190.9 18.9 %collective-permute-start.24 = (f32[128,2]{0,1:T(2,128)S(1)}, f32[128,2]{0,1:T(2,128)S(1)}, u32[]{:S(2)}, u32[]{:S(2)}) collective-permute-start(f32[128,2]{0,1:T(2,128)S(1)} %get-tuple-element.15), channel_id=1, source_target_pairs={{0,64},{64,128},{128,192},{192,256},{256,320},{320,384},{384,448},... | collective-permute-start | bytes 3080 | tf_op jit(solution)/shard_map/ppermute | solution.py:16
  197.6 25.2 %collective-permute-start.10 = (f32[128,2]{0,1:T(2,128)S(1)}, f32[128,2]{0,1:T(2,128)S(1)}, u32[]{:S(2)}, u32[]{:S(2)}) collective-permute-start(f32[128,2]{0,1:T(2,128)S(1)} %max.23), channel_id=1, source_target_pairs={{0,64},{64,128},{128,192},{192,256},{256,320},{320,384},{384,448},... | collective-permute-start | bytes 3080 | tf_op jit(solution)/shard_map/ppermute | solution.py:16
  209.8 5.0 copy-start.13
  210.4 25.2 %collective-permute-start.9 = (f32[128,2,512]{2,0,1:T(8,128)S(1)}, f32[128,2,512]{2,0,1:T(8,128)S(1)}, u32[]{:S(2)}, u32[]{:S(2)}) collective-permute-start(f32[128,2,512]{2,0,1:T(8,128)S(1)} %multiply_add_fusion.4), channel_id=1, source_target_pairs={{0,64},{64,128},{128,192},{192,256},{256,320},{320,384},{384,448},... | collective-permute-start | bytes 1572872 | tf_op jit(solution)/shard_map/ppermute | solution.py:16
  215.6 20.1 %collective-permute-start.25 = (f32[128,2]{0,1:T(2,128)S(1)}, f32[128,2]{0,1:T(2,128)S(1)}, u32[]{:S(2)}, u32[]{:S(2)}) collective-permute-start(f32[128,2]{0,1:T(2,128)S(1)} %get-tuple-element.13), channel_id=1, source_target_pairs={{0,64},{64,128},{128,192},{192,256},{256,320},{320,384},{384,448},... | collective-permute-start | bytes 3080 | tf_op jit(solution)/shard_map/ppermute | solution.py:16
  222.9 24.6 %collective-permute-start.13 = (f32[128,2]{0,1:T(2,128)S(1)}, f32[128,2]{0,1:T(2,128)S(1)}, u32[]{:S(2)}, u32[]{:S(2)}) collective-permute-start(f32[128,2]{0,1:T(2,128)S(1)} %max.24), channel_id=1, source_target_pairs={{0,64},{64,128},{128,192},{192,256},{256,320},{320,384},{384,448},... | collective-permute-start | bytes 3080 | tf_op jit(solution)/shard_map/ppermute | solution.py:16
  235.7 4.5 copy-start.11
  236.2 23.5 %collective-permute-start.12 = (f32[128,2,512]{2,0,1:T(8,128)S(1)}, f32[128,2,512]{2,0,1:T(8,128)S(1)}, u32[]{:S(2)}, u32[]{:S(2)}) collective-permute-start(f32[128,2,512]{2,0,1:T(8,128)S(1)} %multiply_add_fusion.3), channel_id=1, source_target_pairs={{0,64},{64,128},{128,192},{192,256},{256,320},{320,384},{384,448},... | collective-permute-start | bytes 1572872 | tf_op jit(solution)/shard_map/ppermute | solution.py:16
  240.8 18.9 %collective-permute-start.26 = (f32[128,2]{0,1:T(2,128)S(1)}, f32[128,2]{0,1:T(2,128)S(1)}, u32[]{:S(2)}, u32[]{:S(2)}) collective-permute-start(f32[128,2]{0,1:T(2,128)S(1)} %get-tuple-element.11), channel_id=1, source_target_pairs={{0,64},{64,128},{128,192},{192,256},{256,320},{320,384},{384,448},... | collective-permute-start | bytes 3080 | tf_op jit(solution)/shard_map/ppermute | solution.py:16
  247.6 26.2 %collective-permute-start.16 = (f32[128,2]{0,1:T(2,128)S(1)}, f32[128,2]{0,1:T(2,128)S(1)}, u32[]{:S(2)}, u32[]{:S(2)}) collective-permute-start(f32[128,2]{0,1:T(2,128)S(1)} %max.25), channel_id=1, source_target_pairs={{0,64},{64,128},{128,192},{192,256},{256,320},{320,384},{384,448},... | collective-permute-start | bytes 3080 | tf_op jit(solution)/shard_map/ppermute | solution.py:16
  260.3 25.2 %collective-permute-start.15 = (f32[128,2,512]{2,0,1:T(8,128)S(1)}, f32[128,2,512]{2,0,1:T(8,128)S(1)}, u32[]{:S(2)}, u32[]{:S(2)}) collective-permute-start(f32[128,2,512]{2,0,1:T(8,128)S(1)} %multiply_add_fusion.2), channel_id=1, source_target_pairs={{0,64},{64,128},{128,192},{192,256},{256,320},{320,384},{384,448},... | collective-permute-start | bytes 1572872 | tf_op jit(solution)/shard_map/ppermute | solution.py:16
  266.5 19.1 %collective-permute-start.27 = (f32[128,2]{0,1:T(2,128)S(1)}, f32[128,2]{0,1:T(2,128)S(1)}, u32[]{:S(2)}, u32[]{:S(2)}) collective-permute-start(f32[128,2]{0,1:T(2,128)S(1)} %get-tuple-element.9), channel_id=1, source_target_pairs={{0,64},{64,128},{128,192},{192,256},{256,320},{320,384},{384,448},... | collective-permute-start | bytes 3080 | tf_op jit(solution)/shard_map/ppermute | solution.py:16
  273.8 24.6 %collective-permute-start.19 = (f32[128,2]{0,1:T(2,128)S(1)}, f32[128,2]{0,1:T(2,128)S(1)}, u32[]{:S(2)}, u32[]{:S(2)}) collective-permute-start(f32[128,2]{0,1:T(2,128)S(1)} %max.26), channel_id=1, source_target_pairs={{0,64},{64,128},{128,192},{192,256},{256,320},{320,384},{384,448},... | collective-permute-start | bytes 3080 | tf_op jit(solution)/shard_map/ppermute | solution.py:16
  286.2 23.5 %collective-permute-start.18 = (f32[128,2,512]{2,0,1:T(8,128)S(1)}, f32[128,2,512]{2,0,1:T(8,128)S(1)}, u32[]{:S(2)}, u32[]{:S(2)}) collective-permute-start(f32[128,2,512]{2,0,1:T(8,128)S(1)} %multiply_add_fusion.1), channel_id=1, source_target_pairs={{0,64},{64,128},{128,192},{192,256},{256,320},{320,384},{384,448},... | collective-permute-start | bytes 1572872 | tf_op jit(solution)/shard_map/ppermute | solution.py:16
  291.7 17.9 %collective-permute-start.28 = (f32[128,2]{0,1:T(2,128)S(1)}, f32[128,2]{0,1:T(2,128)S(1)}, u32[]{:S(2)}, u32[]{:S(2)}) collective-permute-start(f32[128,2]{0,1:T(2,128)S(1)} %get-tuple-element.7), channel_id=1, source_target_pairs={{0,64},{64,128},{128,192},{192,256},{256,320},{320,384},{384,448},... | collective-permute-start | bytes 3080 | tf_op jit(solution)/shard_map/ppermute | solution.py:16
  310.2 19.4 %collective-permute-start.21 = (f32[128,2,512]{2,0,1:T(8,128)S(1)}, f32[128,2,512]{2,0,1:T(8,128)S(1)}, u32[]{:S(2)}, u32[]{:S(2)}) collective-permute-start(f32[128,2,512]{2,0,1:T(8,128)S(1)} %multiply_add_fusion), channel_id=1, source_target_pairs={{0,64},{64,128},{128,192},{192,256},{256,320},{320,384},{384,448},... | collective-permute-start | bytes 1572872 | tf_op jit(solution)/shard_map/ppermute | solution.py:16
  314.7 14.9 %collective-permute-start.29 = (f32[128,2]{0,1:T(2,128)S(1)}, f32[128,2]{0,1:T(2,128)S(1)}, u32[]{:S(2)}, u32[]{:S(2)}) collective-permute-start(f32[128,2]{0,1:T(2,128)S(1)} %get-tuple-element.5), channel_id=1, source_target_pairs={{0,64},{64,128},{128,192},{192,256},{256,320},{320,384},{384,448},... | collective-permute-start | bytes 3080 | tf_op jit(solution)/shard_map/ppermute | solution.py:16
Sparse Core Ops, SparseCore 0:
  14.6 19.3 all-gather.1
where the time goes:
time: 596 us; the launch traced here: 595 us
  blocking collectives  252 us (42%)
  starting transfers between devices  152 us (26%)
  waiting for transfers between devices  148 us (25%)
  matrix products  17.5 us (3%)
  between operations  14.9 us (2%)
    psum x1, blocking collectives, body(): summed = lax.psum(partial_out, 'head')  252 us
    ppermute x30, starting transfers between devices, from_behind(): return lax.ppermute(value, axis, pairs)  152 us
    ppermute x30, waiting for transfers between devices, from_behind(): return lax.ppermute(value, axis, pairs)  148 us
  transfers between devices with their start and end apart: 31, of which 14 were waited for; matrix products, arithmetic and copies ran while one was open for 3% of the time, Pallas kernels for 0%

commit v1 on v0

v1 whole, which is shorter than its diff:
```python
import jax
import jax.numpy as jnp
from jax import lax
from jax.experimental import pallas as pl
from jax.experimental.pallas import tpu as pltpu
from jax.sharding import PartitionSpec as P

MESH = pl.DeviceIdType.MESH
LAT = 512
VH = 128
UNIT = 32
SCALE = 192.0 ** -0.5 * 1.4426950408889634
NEG = -1e30
F32 = jnp.float32
BF16 = jnp.bfloat16


def place():
    c, h, p = lax.axis_index("ctx"), lax.axis_index("head"), lax.axis_index("pool")
    return c // 2, c % 2, h // 4, h % 4, p


def device(x, yh, z, yl, p):
    return {"ctx": x * 2 + yh, "head": z * 4 + yl, "pool": p}


def greet(others):
    barrier = pltpu.get_barrier_semaphore()
    for other in others:
        pl.semaphore_signal(barrier, inc=1, device_id=other, device_id_type=MESH)
    pl.semaphore_wait(barrier, len(others))


def remote(src, dst, send, recv, to):
    return pltpu.make_async_remote_copy(
        src_ref=src, dst_ref=dst, send_sem=send, recv_sem=recv, device_id=to, device_id_type=MESH
    )


def attention_kernel(
    blocks, cached_ref, q_in, new_in, pool_in, w_uv,
    out,
    qbuf, pbuf, kbuf, vt, wt, acc, stat, ores, orecv, srecv,
    lsem, psem, qs, qr, ups, upr, dns, dnr, zus, zur, zds, zdr, os_, or_, ss, sr,
):
    x, yh, z, yl, p = place()
    b = z % 2
    xu, xd, xo = (x + 1) % 4, (x + 3) % 4, (x + 2) % 4
    at_core = device(x, yh, z, yl, 1 - p)
    at_xu, at_xd, at_xo = [device(k, yh, z, yl, p) for k in (xu, xd, xo)]
    y_up, y_dn = (yh * 4 + yl + 1) % 8, (yh * 4 + yl + 7) % 8
    at_yu, at_yd = [device(x, k // 4, z, k % 4, p) for k in (y_up, y_dn)]
    at_zu, at_zd = [device(x, yh, k % 8, yl, p) for k in (z + 1, z + 7)]
    cached = cached_ref[0]
    half = 16

    mine = pl.ds(p * half, half)
    local = [
        pltpu.make_async_copy(pool_in, pbuf.at[mine], lsem.at[0]),
        pltpu.make_async_copy(q_in, qbuf.at[0], lsem.at[1]),
        pltpu.make_async_copy(new_in, kbuf.at[0, pl.ds(32, 4)], lsem.at[2]),
    ]
    for copy in local:
        copy.start()
    greet([at_core, at_xu, at_xd, at_xo, at_yu, at_yd, at_zu, at_zd])

    push = remote(pool_in, pbuf.at[mine], psem.at[0], psem.at[1], at_core)
    push.start()
    q_up = remote(q_in, qbuf.at[1], qs.at[0], qr.at[0], at_xu)
    q_dn = remote(q_in, qbuf.at[2], qs.at[1], qr.at[1], at_xd)
    q_up.start()
    q_dn.start()
    q_up2 = remote(qbuf.at[1, pl.ds(0, 128)], qbuf.at[3, pl.ds(0, 128)], qs.at[2], qr.at[2], at_xu)
    q_dn2 = remote(qbuf.at[2, pl.ds(128, 128)], qbuf.at[3, pl.ds(128, 128)], qs.at[3], qr.at[3], at_xd)

    for h in range(2):
        wt[h] = w_uv[h].T

    for copy in local:
        copy.wait()
    push.wait_recv()

    def gather(k, carry):
        kbuf[0, pl.ds(2 * k, 2)] = pbuf[blocks[k]].reshape(2, UNIT, kbuf.shape[-1])
        return carry

    lax.fori_loop(0, half, gather, 0)

    def y_up_copy(s, j):
        u = b * 18 + j
        return remote(kbuf.at[s, u], kbuf.at[1, u], ups.at[j], upr.at[j], at_yu)

    def y_dn_copy(s, j):
        u = b * 18 + 9 + j
        return remote(kbuf.at[s, u], kbuf.at[1, u], dns.at[j], dnr.at[j], at_yd)

    def z_up_copy(j, base):
        u = base * 18 + j
        return remote(kbuf.at[1, u], kbuf.at[1, u], zus.at[j], zur.at[j], at_zu)

    def z_dn_copy(j, base):
        u = base * 18 + 9 + j
        return remote(kbuf.at[1, u], kbuf.at[1, u], zds.at[j], zdr.at[j], at_zd)

    @pl.when(yl == 3)
    def _():
        for j in range(9):
            y_up_copy(0, j).start()

    @pl.when(yl == 0)
    def _():
        for j in range(9):
            y_dn_copy(0, j).start()

    def forward(j):
        y_up_copy(1, j).wait_recv()

        @pl.when(yl != 3)
        def _():
            y_up_copy(1, j).start()

        z_up_copy(j, b).start()
        y_dn_copy(1, j).wait_recv()

        @pl.when(yl != 0)
        def _():
            y_dn_copy(1, j).start()

        z_dn_copy(j, b).start()

    owners = [x, xd, xu, xo]

    def scores(keys, query, owner, c, first_row):
        s = lax.dot_general(keys, query, (((1,), (1,)), ((), ())), preferred_element_type=F32) * SCALE
        rows = keys.shape[0]
        parts = []
        hist = min(rows, 1024 - first_row)
        if hist:
            row = lax.broadcasted_iota(jnp.int32, (hist, 256), 0)
            parts.append(jnp.where(row < cached - c * 1024 - first_row, s[:hist], NEG))
        if rows - hist:
            row = lax.broadcasted_iota(jnp.int32, (rows - hist, 256), 0)
            token = lax.broadcasted_iota(jnp.int32, (rows - hist, 256), 1) % 128
            parts.append(jnp.where(row - token <= (owner * 2 + yh - c) * 128, s[hist:], NEG))
        return jnp.concatenate(parts, axis=0) if len(parts) > 1 else parts[0]

    def attend(g, owner, s_at, c, unit, units, fresh):
        rows = units * UNIT
        keys = kbuf[s_at, unit:unit + units].reshape(rows, kbuf.shape[-1])
        s = scores(keys, qbuf[g], owner, c, unit * UNIT)
        top = jnp.max(s, axis=0, keepdims=True)
        if not fresh:
            old = stat[g, 0:1]
            top = jnp.maximum(top, old)
        w = jnp.exp2(s - top)
        total = jnp.sum(w, axis=0, keepdims=True)
        o = jnp.dot(vt[s_at, :, unit * UNIT:unit * UNIT + rows], w.astype(BF16), preferred_element_type=F32)
        if not fresh:
            f = jnp.exp2(old - top)
            total = total + f * stat[g, 1:2]
            o = o + f * acc[g]
        stat[g, 0:1] = top
        stat[g, 1:2] = total
        acc[g] = o

    def turn(s_at, unit, units):
        rows = units * UNIT
        v = kbuf[s_at, unit:unit + units].reshape(rows, kbuf.shape[-1])[:, :LAT]
        vt[s_at, :, unit * UNIT:unit * UNIT + rows] = v.T

    c_own, c_far = x * 2 + yh, x * 2 + 1 - yh
    stat[...] = jnp.zeros_like(stat)
    turn(0, 0, 36)
    forward(0)
    forward(1)
    attend(0, owners[0], 0, c_own, 0, 36, True)
    forward(2)
    forward(3)
    q_up.wait_recv()
    q_up2.start()
    q_dn.wait_recv()
    q_dn2.start()
    forward(4)
    attend(1, owners[1], 0, c_own, 0, 36, True)
    forward(5)
    attend(2, owners[2], 0, c_own, 0, 36, True)
    forward(6)
    q_up2.wait_recv()
    q_dn2.wait_recv()
    attend(3, owners[3], 0, c_own, 0, 36, True)
    forward(7)
    forward(8)
    for j in range(9):
        z_up_copy(j, 1 - b).wait_recv()
        z_dn_copy(j, 1 - b).wait_recv()
    turn(1, 0, 36)

    results = []
    for slot, g in enumerate((3, 1, 2, 0)):
        attend(g, owners[g], 1, c_far, 0, 36, False)
        lat = (acc[g] / stat[g, 1:2]).astype(BF16)
        for h in range(2):
            o = jnp.dot(wt[h], lat[:, h * 128:(h + 1) * 128], preferred_element_type=F32)
            ores[g, :, h * 128:(h + 1) * 128] = o.astype(BF16)
        if g:
            to = {1: at_xd, 2: at_xu, 3: at_xo}[g]
            sent = [
                remote(ores.at[g], orecv.at[g - 1], os_.at[g - 1], or_.at[g - 1], to),
                remote(stat.at[g], srecv.at[g - 1], ss.at[g - 1], sr.at[g - 1], to),
            ]
            for copy in sent:
                copy.start()
            results += sent

    for copy in results:
        copy.wait_recv()
    tops = [stat[0, 0:1]] + [srecv[i, 0:1] for i in range(3)]
    sums = [stat[0, 1:2]] + [srecv[i, 1:2] for i in range(3)]
    outs = [ores[0]] + [orecv[i] for i in range(3)]
    top = jnp.maximum(jnp.maximum(tops[0], tops[1]), jnp.maximum(tops[2], tops[3]))
    shares = [t * jnp.exp2(m - top) for m, t in zip(tops, sums)]
    inv = 1.0 / (shares[0] + shares[1] + shares[2] + shares[3])
    head = sum(o.astype(F32) * (s * inv) for o, s in zip(outs, shares))
    for h in range(2):
        out[:, h * 128:(h + 1) * 128] = head[:, h * 128:(h + 1) * 128].T.astype(BF16)

    push.wait_send()
    for copy in (q_up, q_dn, q_up2, q_dn2):
        copy.wait_send()
    for j in range(9):
        y_up_copy(1, j).wait_send()
        y_dn_copy(1, j).wait_send()
        z_up_copy(j, b).wait_send()
        z_dn_copy(j, b).wait_send()
    for copy in results:
        copy.wait_send()


def attention(blocks, cached, q, new, pool, w_uv):
    width = q.shape[-1]
    any_ = pl.BlockSpec(memory_space=pl.ANY)
    smem = pl.BlockSpec(memory_space=pltpu.SMEM)
    vmem = pl.BlockSpec(memory_space=pltpu.VMEM)
    dma = pltpu.SemaphoreType.DMA
    return pl.pallas_call(
        attention_kernel,
        out_shape=jax.ShapeDtypeStruct((128, 256), BF16),
        in_specs=[smem, smem, any_, any_, any_, vmem],
        out_specs=vmem,
        scratch_shapes=[
            pltpu.VMEM((4, 256, width), BF16),
            pltpu.VMEM((32, 64, width), BF16),
            pltpu.VMEM((2, 36, UNIT, width), BF16),
            pltpu.VMEM((2, LAT, 36 * UNIT), BF16),
            pltpu.VMEM((2, VH, LAT), BF16),
            pltpu.VMEM((4, LAT, 256), F32),
            pltpu.VMEM((4, 8, 256), F32),
            pltpu.VMEM((4, VH, 256), BF16),
            pltpu.VMEM((3, VH, 256), BF16),
            pltpu.VMEM((3, 8, 256), F32),
            dma((3,)), dma((2,)), dma((4,)), dma((4,)),
            dma((9,)), dma((9,)), dma((9,)), dma((9,)),
            dma((9,)), dma((9,)), dma((9,)), dma((9,)),
            dma((3,)), dma((3,)), dma((3,)), dma((3,)),
        ],
        compiler_params=pltpu.CompilerParams(
            collective_id=0, has_side_effects=True, vmem_limit_bytes=48 * 2**20
        ),
        cost_estimate=pl.CostEstimate(flops=5 * 10**9, bytes_accessed=4 * 10**6, transcendentals=2 * 10**6),
    )(blocks, cached, q, new, pool, w_uv)


def project_kernel(
    a_ref, w_in, out,
    w, up_out, up_in, dn_out, dn_in, own, y_out, y_in,
    wsem, us, ur, ds, dr, ys, yr,
):
    x, yh, z, yl, p = place()
    at_zu, at_zd = [device(x, yh, k % 8, yl, p) for k in (z + 1, z + 7)]
    at_y = [device(x, yh, z, (yl + d) % 4, p) for d in (1, 2, 3)]
    load = pltpu.make_async_copy(w_in, w, wsem)
    load.start()
    greet([at_zu, at_zd] + at_y)
    load.wait()
    a = a_ref[...]

    def term(dest):
        at = pl.multiple_of((dest % 8) * 896, 128)
        return jnp.dot(a, w[:, pl.ds(at, 896)], preferred_element_type=F32)

    def up(s, r):
        rows = pl.ds(r * 32, 32)
        return remote(up_out.at[s, rows], up_in.at[s, rows], us.at[s, r], ur.at[s, r], at_zu)

    def dn(s, r):
        rows = pl.ds(r * 32, 32)
        return remote(dn_out.at[s, rows], dn_in.at[s, rows], ds.at[s, r], dr.at[s, r], at_zd)

    up_order, dn_order = (2, 3, 0, 1), (0, 1, 2, 3)
    started = []
    for s in range(4):
        if s == 0:
            far = term(z + 4)
            for r in (0, 1):
                up_out[0, r * 32:(r + 1) * 32] = far[r * 32:(r + 1) * 32].astype(BF16)
                started.append(up(0, r))
                started[-1].start()
                r = r + 2
                dn_out[0, r * 32:(r + 1) * 32] = far[r * 32:(r + 1) * 32].astype(BF16)
                started.append(dn(0, r))
                started[-1].start()
            continue
        t_up, t_dn = term(z + 4 - s), term(z + 4 + s)
        for i in range(4):
            for flow, order, t, sent, got, extra in (
                (up, up_order, t_up, up_out, up_in, (0, 1)),
                (dn, dn_order, t_dn, dn_out, dn_in, (2, 3)),
            ):
                r = order[i]
                rows = slice(r * 32, (r + 1) * 32)
                v = t[rows]
                if s > 1 or r in extra:
                    flow(s - 1, r).wait_recv()
                    v = v + got[s - 1, rows].astype(F32)
                sent[s, rows] = v.astype(BF16)
                started.append(flow(s, r))
                started[-1].start()

    t = term(z)
    y_copies = []
    for r in range(4):
        rows = slice(r * 32, (r + 1) * 32)
        up(3, r).wait_recv()
        dn(3, r).wait_recv()
        v = t[rows] + up_in[3, rows].astype(F32) + dn_in[3, rows].astype(F32)
        for k in range(4):
            piece = v[:, k * 224:(k + 1) * 224]
            own[k, rows, 0:224] = piece
            y_out[k, rows, 0:224] = piece.astype(BF16)
        for d in range(3):
            at = pl.ds(r * 32, 32)
            copy = remote(
                y_out.at[(yl + d + 1) % 4, at], y_in.at[d, at], ys.at[d, r], yr.at[d, r], at_y[d]
            )
            copy.start()
            y_copies.append(copy)
    for r in range(4):
        rows = slice(r * 32, (r + 1) * 32)
        for d in range(3):
            y_copies[r * 3 + d].wait_recv()
        v = own[yl, rows, 0:224]
        for d in range(3):
            v = v + y_in[d, rows, 0:224].astype(F32)
        out[rows, :] = v.astype(BF16)
    for copy in started + y_copies:
        copy.wait_send()


def project(a, w_o):
    any_ = pl.BlockSpec(memory_space=pl.ANY)
    vmem = pl.BlockSpec(memory_space=pltpu.VMEM)
    dma = pltpu.SemaphoreType.DMA
    return pl.pallas_call(
        project_kernel,
        out_shape=jax.ShapeDtypeStruct((128, 224), BF16),
        in_specs=[vmem, any_],
        out_specs=vmem,
        scratch_shapes=[
            pltpu.VMEM(w_o.shape, BF16),
            pltpu.VMEM((4, 128, 896), BF16),
            pltpu.VMEM((4, 128, 896), BF16),
            pltpu.VMEM((4, 128, 896), BF16),
            pltpu.VMEM((4, 128, 896), BF16),
            pltpu.VMEM((4, 128, 256), F32),
            pltpu.VMEM((4, 128, 256), BF16),
            pltpu.VMEM((3, 128, 256), BF16),
            dma, dma((4, 4)), dma((4, 4)), dma((4, 4)), dma((4, 4)), dma((3, 4)), dma((3, 4)),
        ],
        compiler_params=pltpu.CompilerParams(
            collective_id=1, has_side_effects=True, vmem_limit_bytes=48 * 2**20
        ),
        cost_estimate=pl.CostEstimate(flops=5 * 10**8, bytes_accessed=4 * 10**6, transcendentals=0),
    )(a, w_o)


def body(queries, new_latent, cache_pool, block_list, cached_lengths, w_uv, w_o):
    width = queries.shape[-1]
    q = jnp.transpose(queries[0], (1, 0, 2)).reshape(256, width)
    new = new_latent[0].reshape(4, UNIT, width)
    a = attention(block_list[0, 0], cached_lengths, q, new, cache_pool[0], w_uv)
    return project(a, w_o.reshape(256, -1))[None]


def solution(mesh):
    in_specs = (
        P("pool", "ctx", "head", None),
        P("pool", "ctx", None),
        P("ctx", "pool", None, None),
        P("pool", "ctx", None),
        P("pool"),
        P("head", None, None),
        P("head", None, None),
    )
    out_specs = P("pool", "ctx", "head")
    return jax.shard_map(body, mesh=mesh, in_specs=in_specs, out_specs=out_specs, check_vma=False)
```

time: 596 us -> 235 us (0.39)
  the two profiles are of different devices: /device:TPU:6 before, /device:TPU:56 now
where the time goes in v1:
time: 235 us; the launch traced here: 234 us
  Pallas kernels  228 us (97%)
  local copies, waits for them, and re-layouts  5.87 us (2%)
    pallas_call x1, Pallas kernels, attention(): pl.pallas_call(attention_kernel, out_shape=jax.ShapeDtypeStruct((128, 256...  196 us
    pallas_call x1, Pallas kernels, project(): pl.pallas_call(project_kernel, out_shape=jax.ShapeDtypeStruct((128, 224),...  31.2 us

profile of v1, /device:TPU:56, one launch (start us, length us, event | category | flops | bytes accessed | tf_op | source)
XLA Modules:
  0.0 234.1 jit_solution(15411073200210654599)
XLA Ops:
  0.7 1.1 copy.9
  1.7 1.2 copy.8
  2.9 0.0 copy-start.1
  2.9 1.3 copy-done.1
  4.2 0.0 copy-start.2
  4.2 0.9 copy-done.2
  5.2 0.0 copy-start.3
  5.2 0.7 copy-done.3
  5.8 0.0 copy-start
  5.8 196.3 %shard_map.73.a_ref = bf16[128,256]{1,0:T(8,128)(2,1)S(1)} custom-call(s32[16]{0:T(128)S(1)} %bitcast.14, s32[1]{0:T(128)S(6)} %copy.11.cached_ref, bf16[256,576]{1,0:T(8,128)(2,1)S(1)} %bitcast.10, bf16[4,32,576]{2,1,0:T(8,128)(2,1)S(1)} %bitcast.12, bf16[16,64,576]{2,1,0:T(8,128)(2,1)S(1)} %bitcast.13, bf16[2,512,128]{2,1,0:T(8,128)(2,1)S(1)} %copy-done.2), custom_call_target="tpu_custom_call" | custom-call | flops 5000000000 | bytes 4000000 | tf_op jit(solution)/shard_map/pallas_call | solution.py:245
  202.1 0.0 copy-done
  202.1 31.2 %shard_map.74 = bf16[128,224]{1,0:T(8,128)(2,1)S(1)} custom-call(bf16[128,256]{1,0:T(8,128)(2,1)S(1)} %shard_map.73.a_ref, bf16[256,7168]{1,0:T(8,128)(2,1)S(1)} %bitcast.9), custom_call_target="tpu_custom_call" | custom-call | flops 500000000 | bytes 4000000 | tf_op jit(solution)/shard_map/pallas_call | solution.py:363
  233.4 0.7 copy.10
Async XLA Ops:
  2.9 1.3 copy-start.1
  4.2 0.9 copy-start.2
  5.2 0.7 copy-start.3
  5.8 196.3 %copy-start = (bf16[2,128,7168]{2,1,0:T(8,128)(2,1)S(1)}, bf16[2,128,7168]{2,1,0:T(8,128)(2,1)}, u32[]{:S(2)}) copy-start(bf16[2,128,7168]{2,1,0:T(8,128)(2,1)} %param.13) | copy-start | bytes 11010052

commit v2 on v0

v2 whole, which is shorter than its diff:
```python
import jax
import jax.numpy as jnp
from jax import lax
from jax.experimental import pallas as pl
from jax.experimental.pallas import tpu as pltpu
from jax.sharding import PartitionSpec as P

MESH = pl.DeviceIdType.MESH
LAT = 512
VH = 128
UNIT = 32
SCALE = 192.0 ** -0.5 * 1.4426950408889634
NEG = -1e30
F32 = jnp.float32
BF16 = jnp.bfloat16


def place():
    c, h, p = lax.axis_index("ctx"), lax.axis_index("head"), lax.axis_index("pool")
    return c // 2, c % 2, h // 4, h % 4, p


def device(x, yh, z, yl, p):
    return {"ctx": x * 2 + yh, "head": z * 4 + yl, "pool": p}


def greet(others):
    barrier = pltpu.get_barrier_semaphore()
    for other in others:
        pl.semaphore_signal(barrier, inc=1, device_id=other, device_id_type=MESH)
    pl.semaphore_wait(barrier, len(others))


def remote(src, dst, send, recv, to):
    return pltpu.make_async_remote_copy(
        src_ref=src, dst_ref=dst, send_sem=send, recv_sem=recv, device_id=to, device_id_type=MESH
    )


def kernel(
    blocks, cached_ref, q_in, new_in, pool_in, w_uv, w_in,
    out,
    qbuf, pbuf, kbuf, newt, vt, wt, acc, stat, ores, orecv, sstat, srecv,
    w, wo, at, up_out, up_in, dn_out, dn_in, own, y_out, y_in,
    lsem, psem, qs, qr, ups, upr, dns, dnr, zus, zur, zds, zdr, os_, or_, ss, sr,
    us, ur, ds, dr, ys, yr,
):
    x, yh, z, yl, p = place()
    b = z % 2
    xu, xd, xo = (x + 1) % 4, (x + 3) % 4, (x + 2) % 4
    at_core = device(x, yh, z, yl, 1 - p)
    at_xu, at_xd, at_xo = [device(k, yh, z, yl, p) for k in (xu, xd, xo)]
    y_up, y_dn = (yh * 4 + yl + 1) % 8, (yh * 4 + yl + 7) % 8
    at_yu, at_yd = [device(x, k // 4, z, k % 4, p) for k in (y_up, y_dn)]
    at_zu, at_zd = [device(x, yh, k % 8, yl, p) for k in (z + 1, z + 7)]
    at_y = [device(x, yh, z, (yl + d) % 4, p) for d in (1, 2, 3)]
    cached = cached_ref[0]
    width = kbuf.shape[-1]
    half = 16

    mine = pl.ds(p * half, half)
    local = [
        pltpu.make_async_copy(pool_in, pbuf.at[mine], lsem.at[0]),
        pltpu.make_async_copy(q_in, qbuf.at[0], lsem.at[1]),
        pltpu.make_async_copy(new_in, newt, lsem.at[2]),
    ]
    load_w = pltpu.make_async_copy(w_in, w, lsem.at[3])
    load_uv = pltpu.make_async_copy(w_uv, wt, lsem.at[4])
    for copy in local + [load_uv, load_w]:
        copy.start()
    greet([at_core, at_xu, at_xd, at_xo, at_yu, at_yd, at_zu, at_zd] + at_y)

    push = remote(pool_in, pbuf.at[mine], psem.at[0], psem.at[1], at_core)
    push.start()
    q_up = remote(q_in, qbuf.at[1], qs.at[0], qr.at[0], at_xu)
    q_dn = remote(q_in, qbuf.at[2], qs.at[1], qr.at[1], at_xd)
    q_up.start()
    q_dn.start()
    q_up2 = remote(qbuf.at[1, 0], qbuf.at[3, 0], qs.at[2], qr.at[2], at_xu)
    q_dn2 = remote(qbuf.at[2, 1], qbuf.at[3, 1], qs.at[3], qr.at[3], at_xd)

    for copy in local:
        copy.wait()
    kbuf[0, 32:36] = newt[...].T.reshape(4, UNIT, width)
    push.wait_recv()

    def gather(k, carry):
        kbuf[0, pl.ds(2 * k, 2)] = pbuf[blocks[k]].reshape(2, UNIT, width)
        return carry

    lax.fori_loop(0, half, gather, 0)

    def y_up_copy(s, j):
        u = j * 4 + b * 2
        return remote(kbuf.at[s, u], kbuf.at[1, u], ups.at[j], upr.at[j], at_yu)

    def y_dn_copy(s, j):
        u = j * 4 + b * 2 + 1
        return remote(kbuf.at[s, u], kbuf.at[1, u], dns.at[j], dnr.at[j], at_yd)

    def z_up_copy(j, base):
        u = j * 4 + base * 2
        return remote(kbuf.at[1, u], kbuf.at[1, u], zus.at[j], zur.at[j], at_zu)

    def z_dn_copy(j, base):
        u = j * 4 + base * 2 + 1
        return remote(kbuf.at[1, u], kbuf.at[1, u], zds.at[j], zdr.at[j], at_zd)

    @pl.when(yl == 3)
    def _():
        for j in range(9):
            y_up_copy(0, j).start()

    @pl.when(yl == 0)
    def _():
        for j in range(9):
            y_dn_copy(0, j).start()

    def forward(step):
        j = step - 1 - yl

        @pl.when((j >= 0) & (j < 9))
        def _():
            y_up_copy(1, j).wait_recv()

            @pl.when(yl != 3)
            def _():
                y_up_copy(1, j).start()

            z_up_copy(j, b).start()

        k = step - 4 + yl

        @pl.when((k >= 0) & (k < 9))
        def _():
            y_dn_copy(1, k).wait_recv()

            @pl.when(yl != 0)
            def _():
                y_dn_copy(1, k).start()

            z_dn_copy(k, b).start()

    owners = [x, xd, xu, xo]

    def attend(slots, s_at, tile):
        c = x * 2 + (yh if s_at == 0 else 1 - yh)
        lo, lanes = slots[0] * 256, len(slots) * 256
        cols = slice(lo, lo + lanes)
        units = slice(tile * 12, tile * 12 + 12)
        keys = kbuf[s_at, units].reshape(384, width)
        query = jnp.concatenate([qbuf[g, h] for g in slots for h in range(2)], axis=1)
        s = jnp.dot(keys, query, preferred_element_type=F32) * SCALE
        hist = 384 if tile < 2 else 256
        row = lax.broadcasted_iota(jnp.int32, (hist, lanes), 0)
        s_hist = jnp.where(row < cached - c * 1024 - tile * 384, s[:hist], NEG)
        if tile == 2:
            token = lax.broadcasted_iota(jnp.int32, (1, 256), 1) % 128
            last = jnp.concatenate([token + (owners[g] * 2 + yh - c) * 128 for g in slots], axis=1)
            row = lax.broadcasted_iota(jnp.int32, (128, lanes), 0)
            s = jnp.concatenate([s_hist, jnp.where(row <= last, s[hist:], NEG)], axis=0)
        else:
            s = s_hist
        fresh = s_at == 0 and tile == 0
        top = jnp.max(s, axis=0, keepdims=True)
        if not fresh:
            old = stat[0:1, cols]
            top = jnp.maximum(top, old)
        e = jnp.exp2(s - top)
        total = jnp.sum(e, axis=0, keepdims=True)
        o = jnp.dot(vt[s_at, :, tile * 384:(tile + 1) * 384], e.astype(BF16), preferred_element_type=F32)
        if not fresh:
            f = jnp.exp2(old - top)
            total = total + f * stat[1:2, cols]
            o = o + f * acc[:, cols]
        stat[0:1, cols] = top
        stat[1:2, cols] = total
        acc[:, cols] = o

    def turn(s_at, tile):
        v = kbuf[s_at, tile * 12:tile * 12 + 12].reshape(384, width)[:, :LAT]
        vt[s_at, :, tile * 384:(tile + 1) * 384] = v.T

    def turn_w(i):
        wo[i * 896:(i + 1) * 896] = w[:, i * 896:(i + 1) * 896].T

    near, far = (0, 1), (2, 3)
    for t in range(3):
        turn(0, t)
    forward(1)
    load_w.wait()
    turn_w(0)
    forward(2)
    q_up.wait_recv()
    q_up2.start()
    q_dn.wait_recv()
    q_dn2.start()
    forward(3)
    attend(near, 0, 0)
    forward(4)
    attend(near, 0, 1)
    forward(5)
    attend(near, 0, 2)
    forward(6)
    q_up2.wait_recv()
    q_dn2.wait_recv()
    attend(far, 0, 0)
    forward(7)
    attend(far, 0, 1)
    forward(8)
    attend(far, 0, 2)
    forward(9)
    turn_w(1)
    load_uv.wait()

    def landed(tile):
        for j in range(3 * tile, 3 * tile + 3):
            z_up_copy(j, 1 - b).wait_recv()
            z_dn_copy(j, 1 - b).wait_recv()
        turn(1, tile)

    landed(0)
    attend(near, 1, 0)
    forward(10)
    attend(far, 1, 0)
    forward(11)
    turn_w(2)
    turn_w(3)
    forward(12)
    landed(1)
    attend(near, 1, 1)
    attend(far, 1, 1)
    for i in range(4, 8):
        turn_w(i)
    landed(2)

    results = []
    for slots in (far, near):
        attend(slots, 1, 2)
        for g in reversed(slots):
            cols = slice(g * 256, (g + 1) * 256)
            lat = (acc[:, cols] / stat[1:2, cols]).astype(BF16)
            for h in range(2):
                o = lax.dot_general(
                    wt[h], lat[:, h * 128:(h + 1) * 128], (((0,), (0,)), ((), ())), preferred_element_type=F32
                )
                ores[g, :, h * 128:(h + 1) * 128] = o.astype(BF16)
            if g:
                sstat[g - 1, 0:2] = stat[0:2, cols]
                to = {1: at_xd, 2: at_xu, 3: at_xo}[g]
                sent = [
                    remote(ores.at[g], orecv.at[g - 1], os_.at[g - 1], or_.at[g - 1], to),
                    remote(sstat.at[g - 1], srecv.at[g - 1], ss.at[g - 1], sr.at[g - 1], to),
                ]
                for copy in sent:
                    copy.start()
                results += sent

    for copy in results:
        copy.wait_recv()
    tops = [stat[0:1, 0:256]] + [srecv[i, 0:1] for i in range(3)]
    sums = [stat[1:2, 0:256]] + [srecv[i, 1:2] for i in range(3)]
    outs = [ores[0]] + [orecv[i] for i in range(3)]
    top = jnp.maximum(jnp.maximum(tops[0], tops[1]), jnp.maximum(tops[2], tops[3]))
    shares = [t * jnp.exp2(m - top) for m, t in zip(tops, sums)]
    inv = 1.0 / (shares[0] + shares[1] + shares[2] + shares[3])
    head = sum(o.astype(F32) * (s * inv) for o, s in zip(outs, shares))
    for h in range(2):
        at[h * 128:(h + 1) * 128] = head[:, h * 128:(h + 1) * 128].astype(BF16)

    a = at[...]

    def term(dest, d):
        row = pl.multiple_of((dest % 8) * 896 + ((yl + 1 + d) % 4) * 224, 16)
        return jnp.dot(wo[pl.ds(row, 224)], a, preferred_element_type=F32)

    def up(s, d):
        return remote(up_out.at[s, d], up_in.at[s, d], us.at[s, d], ur.at[s, d], at_zu)

    def dn(s, d):
        return remote(dn_out.at[s, d], dn_in.at[s, d], ds.at[s, d], dr.at[s, d], at_zd)

    started = []
    for s in range(4):
        for d in range(4):
            for flow, dest, sent, got, extra in (
                (up, z + 4 - s, up_out, up_in, (2, 3)),
                (dn, z + 4 + s, dn_out, dn_in, (0, 1)),
            ):
                if s == 0 and d not in extra:
                    continue
                v = term(dest, d)
                if s > 1 or (s == 1 and d in extra):
                    flow(s - 1, d).wait_recv()
                    v = v + got[s - 1, d].astype(F32)
                sent[s, d] = v.astype(BF16)
                started.append(flow(s, d))
                started[-1].start()

    for d in range(4):
        v = term(z, d)
        up(3, d).wait_recv()
        dn(3, d).wait_recv()
        v = v + up_in[3, d].astype(F32) + dn_in[3, d].astype(F32)
        if d < 3:
            y_out[d] = v.astype(BF16)
            copy = remote(y_out.at[d], y_in.at[d], ys.at[d], yr.at[d], at_y[d])
            copy.start()
            started.append(copy)
        else:
            own[...] = v
    v = own[...]
    for d in range(3):
        started[d - 3].wait_recv()
        v = v + y_in[d].astype(F32)
    out[...] = v.astype(BF16)

    push.wait_send()
    for copy in (q_up, q_dn, q_up2, q_dn2):
        copy.wait_send()
    for j in range(9):
        y_up_copy(1, j).wait_send()
        y_dn_copy(1, j).wait_send()
        z_up_copy(j, b).wait_send()
        z_dn_copy(j, b).wait_send()
    for copy in results + started:
        copy.wait_send()


def body(queries, new_latent, cache_pool, block_list, cached_lengths, w_uv, w_o):
    width = queries.shape[-1]
    columns = w_o.shape[-1]
    q = jnp.transpose(queries[0], (1, 2, 0))
    new = new_latent[0].T
    hbm = pl.BlockSpec(memory_space=pltpu.HBM)
    smem = pl.BlockSpec(memory_space=pltpu.SMEM)
    dma = pltpu.SemaphoreType.DMA
    mixed = pl.pallas_call(
        kernel,
        out_shape=jax.ShapeDtypeStruct((224, 128), BF16),
        in_specs=[smem, smem, hbm, hbm, hbm, hbm, hbm],
        out_specs=pl.BlockSpec(memory_space=pltpu.VMEM),
        scratch_shapes=[
            pltpu.VMEM((4, 2, width, 128), BF16),
            pltpu.VMEM((32, 64, width), BF16),
            pltpu.VMEM((2, 36, UNIT, width), BF16),
            pltpu.VMEM((width, 128), BF16),
            pltpu.VMEM((2, LAT, 36 * UNIT), BF16),
            pltpu.VMEM((2, LAT, VH), BF16),
            pltpu.VMEM((LAT, 1024), F32),
            pltpu.VMEM((8, 1024), F32),
            pltpu.VMEM((4, VH, 256), BF16),
            pltpu.VMEM((3, VH, 256), BF16),
            pltpu.VMEM((3, 8, 256), F32),
            pltpu.VMEM((3, 8, 256), F32),
            pltpu.VMEM((256, columns), BF16),
            pltpu.VMEM((columns, 256), BF16),
            pltpu.VMEM((256, 128), BF16),
            pltpu.VMEM((4, 4, 224, 128), BF16),
            pltpu.VMEM((4, 4, 224, 128), BF16),
            pltpu.VMEM((4, 4, 224, 128), BF16),
            pltpu.VMEM((4, 4, 224, 128), BF16),
            pltpu.VMEM((224, 128), F32),
            pltpu.VMEM((3, 224, 128), BF16),
            pltpu.VMEM((3, 224, 128), BF16),
            dma((5,)), dma((2,)), dma((4,)), dma((4,)),
            dma((9,)), dma((9,)), dma((9,)), dma((9,)),
            dma((9,)), dma((9,)), dma((9,)), dma((9,)),
            dma((3,)), dma((3,)), dma((3,)), dma((3,)),
            dma((4, 4)), dma((4, 4)), dma((4, 4)), dma((4, 4)), dma((3,)), dma((3,)),
        ],
        compiler_params=pltpu.CompilerParams(
            collective_id=0, has_side_effects=True, vmem_limit_bytes=56 * 2**20
        ),
        cost_estimate=pl.CostEstimate(flops=6 * 10**9, bytes_accessed=8 * 10**6, transcendentals=2 * 10**6),
    )(block_list[0, 0], cached_lengths, q, new, cache_pool[0], w_uv, w_o.reshape(256, columns))
    return mixed.T[None]


def solution(mesh):
    in_specs = (
        P("pool", "ctx", "head", None),
        P("pool", "ctx", None),
        P("ctx", "pool", None, None),
        P("pool", "ctx", None),
        P("pool"),
        P("head", None, None),
        P("head", None, None),
    )
    out_specs = P("pool", "ctx", "head")
    return jax.shard_map(body, mesh=mesh, in_specs=in_specs, out_specs=out_specs, check_vma=False)
```

time: 596 us -> 85.3 us (0.14)
  the two profiles are of different devices: /device:TPU:6 before, /device:TPU:56 now
where the time goes in v2:
time: 85.3 us; the launch traced here: 85 us
  Pallas kernels  82.9 us (97%)
  local copies, waits for them, and re-layouts  1.45 us (2%)
    pallas_call x1, Pallas kernels, body(): pl.pallas_call(kernel, out_shape=jax.ShapeDtypeStruct((224, 128), BF16),...  82.9 us

profile of v2, /device:TPU:56, one launch (start us, length us, event | category | flops | bytes accessed | tf_op | source)
XLA Modules:
  0.0 85.0 jit_solution(2334919679806142184)
XLA Ops:
  0.7 82.9 %shard_map.73 = bf16[224,128]{1,0:T(8,128)(2,1)} custom-call(s32[16]{0:T(128)} %bitcast.17, s32[1]{0:T(128)S(6)} %copy.9.cached_ref, bf16[2,576,128]{2,1,0:T(8,128)(2,1)} %bitcast.15, bf16[576,128]{1,0:T(8,128)(2,1)} %bitcast.16, bf16[16,64,576]{2,1,0:T(8,128)(2,1)} %bitcast.14, bf16[2,512,128]{2,1,0:T(8,128)(2,1)} %w_uv.1, bf16[256,7168]{1,0:T(8,128)(2,1)} %bitcast.13), custom_call_target="tpu_custom_call" | custom-call | flops 6000000000 | bytes 8000000 | tf_op jit(solution)/shard_map/pallas_call | solution.py:338
  83.5 1.4 %copy.10 = bf16[1,128,224]{1,2,0:T(8,128)(2,1)} copy(bf16[1,128,224]{1,2,0:T(8,128)(2,1)} %bitcast.12) | data formatting | bytes 114688

commit v3 on v2

--- a/solution.py
+++ b/solution.py
@@ -9,6 +9,7 @@
 LAT = 512
 VH = 128
 UNIT = 32
+HOP = 4
 SCALE = 192.0 ** -0.5 * 1.4426950408889634
 NEG = -1e30
 F32 = jnp.float32
@@ -55,7 +56,7 @@
     at_zu, at_zd = [device(x, yh, k % 8, yl, p) for k in (z + 1, z + 7)]
     at_y = [device(x, yh, z, (yl + d) % 4, p) for d in (1, 2, 3)]
     cached = cached_ref[0]
-    width = kbuf.shape[-1]
+    width = q_in.shape[1]
     half = 16
 
     mine = pl.ds(p * half, half)
@@ -72,23 +73,17 @@
 
     push = remote(pool_in, pbuf.at[mine], psem.at[0], psem.at[1], at_core)
     push.start()
-    q_up = remote(q_in, qbuf.at[1], qs.at[0], qr.at[0], at_xu)
-    q_dn = remote(q_in, qbuf.at[2], qs.at[1], qr.at[1], at_xd)
-    q_up.start()
-    q_dn.start()
-    q_up2 = remote(qbuf.at[1, 0], qbuf.at[3, 0], qs.at[2], qr.at[2], at_xu)
-    q_dn2 = remote(qbuf.at[2, 1], qbuf.at[3, 1], qs.at[3], qr.at[3], at_xd)
+    q_up = [remote(q_in.at[h], qbuf.at[1, h], qs.at[h], qr.at[h], at_xu) for h in range(2)]
+    q_dn = [remote(q_in.at[h], qbuf.at[2, h], qs.at[2 + h], qr.at[2 + h], at_xd) for h in range(2)]
+    for copy in (q_up[0], q_dn[1], q_up[1], q_dn[0]):
+        copy.start()
+    q_up2 = remote(qbuf.at[1, 0], qbuf.at[3, 0], qs.at[4], qr.at[4], at_xu)
+    q_dn2 = remote(qbuf.at[2, 1], qbuf.at[3, 1], qs.at[5], qr.at[5], at_xd)
 
     for copy in local:
         copy.wait()
-    kbuf[0, 32:36] = newt[...].T.reshape(4, UNIT, width)
-    push.wait_recv()
-
-    def gather(k, carry):
-        kbuf[0, pl.ds(2 * k, 2)] = pbuf[blocks[k]].reshape(2, UNIT, width)
-        return carry
-
-    lax.fori_loop(0, half, gather, 0)
+    kbuf[0, :, :, width:] = jnp.zeros((36, UNIT, kbuf.shape[-1] - width), BF16)
+    kbuf[0, 0:4, :, :width] = newt[...].T.reshape(4, UNIT, width)
 
     def y_up_copy(s, j):
         u = j * 4 + b * 2
@@ -106,18 +101,29 @@
         u = j * 4 + base * 2 + 1
         return remote(kbuf.at[1, u], kbuf.at[1, u], zds.at[j], zdr.at[j], at_zd)
 
-    @pl.when(yl == 3)
-    def _():
-        for j in range(9):
-            y_up_copy(0, j).start()
-
-    @pl.when(yl == 0)
-    def _():
-        for j in range(9):
-            y_dn_copy(0, j).start()
+    def first(lo, hi):
+        @pl.when(yl == 3)
+        def _():
+            for j in range(lo, hi):
+                y_up_copy(0, j).start()
+
+        @pl.when(yl == 0)
+        def _():
+            for j in range(lo, hi):
+                y_dn_copy(0, j).start()
+
+    first(0, 1)
+    push.wait_recv()
+
+    def gather(k, carry):
+        kbuf[0, pl.ds(2 * k + 4, 2), :, :width] = pbuf[blocks[k]].reshape(2, UNIT, width)
+        return carry
+
+    lax.fori_loop(0, half, gather, 0)
+    first(1, 9)
 
     def forward(step):
-        j = step - 1 - yl
+        j = step - HOP * (yl + 1)
 
         @pl.when((j >= 0) & (j < 9))
         def _():
@@ -129,7 +135,7 @@
 
             z_up_copy(j, b).start()
 
-        k = step - 4 + yl
+        k = step - HOP * (4 - yl)
 
         @pl.when((k >= 0) & (k < 9))
         def _():
@@ -148,17 +154,17 @@
         lo, lanes = slots[0] * 256, len(slots) * 256
         cols = slice(lo, lo + lanes)
         units = slice(tile * 12, tile * 12 + 12)
-        keys = kbuf[s_at, units].reshape(384, width)
+        keys = kbuf[s_at, units].reshape(384, kbuf.shape[-1])[:, :width]
         query = jnp.concatenate([qbuf[g, h] for g in slots for h in range(2)], axis=1)
         s = jnp.dot(keys, query, preferred_element_type=F32) * SCALE
-        hist = 384 if tile < 2 else 256
-        row = lax.broadcasted_iota(jnp.int32, (hist, lanes), 0)
-        s_hist = jnp.where(row < cached - c * 1024 - tile * 384, s[:hist], NEG)
-        if tile == 2:
+        new = 0 if tile else 128
+        row = lax.broadcasted_iota(jnp.int32, (384 - new, lanes), 0)
+        s_hist = jnp.where(row < cached - c * 1024 - (tile * 384 + new - 128), s[new:], NEG)
+        if new:
             token = lax.broadcasted_iota(jnp.int32, (1, 256), 1) % 128
             last = jnp.concatenate([token + (owners[g] * 2 + yh - c) * 128 for g in slots], axis=1)
             row = lax.broadcasted_iota(jnp.int32, (128, lanes), 0)
-            s = jnp.concatenate([s_hist, jnp.where(row <= last, s[hist:], NEG)], axis=0)
+            s = jnp.concatenate([jnp.where(row <= last, s[:new], NEG), s_hist], axis=0)
         else:
             s = s_hist
         fresh = s_at == 0 and tile == 0
@@ -178,7 +184,7 @@
         acc[:, cols] = o
 
     def turn(s_at, tile):
-        v = kbuf[s_at, tile * 12:tile * 12 + 12].reshape(384, width)[:, :LAT]
+        v = kbuf[s_at, tile * 12:tile * 12 + 12].reshape(384, kbuf.shape[-1])[:, :LAT]
         vt[s_at, :, tile * 384:(tile + 1) * 384] = v.T
 
     def turn_w(i):
@@ -187,31 +193,39 @@
     near, far = (0, 1), (2, 3)
     for t in range(3):
         turn(0, t)
-    forward(1)
+    q_up[0].wait_recv()
+    q_up2.start()
+    q_dn[1].wait_recv()
+    q_dn2.start()
     load_w.wait()
+    forward(4)
     turn_w(0)
-    forward(2)
-    q_up.wait_recv()
-    q_up2.start()
-    q_dn.wait_recv()
-    q_dn2.start()
-    forward(3)
+    forward(5)
+    turn_w(1)
+    forward(6)
+    q_up[1].wait_recv()
     attend(near, 0, 0)
-    forward(4)
+    forward(7)
     attend(near, 0, 1)
-    forward(5)
+    forward(8)
     attend(near, 0, 2)
-    forward(6)
+    forward(9)
+    turn_w(2)
+    forward(10)
+    q_dn[0].wait_recv()
     q_up2.wait_recv()
     q_dn2.wait_recv()
     attend(far, 0, 0)
-    forward(7)
+    forward(11)
     attend(far, 0, 1)
-    forward(8)
+    forward(12)
     attend(far, 0, 2)
-    forward(9)
-    turn_w(1)
+    forward(13)
     load_uv.wait()
+    for step in range(14, 25):
+        if step % 2 == 0 and step < 24:
+            turn_w(step // 2 - 4)
+        forward(step)
 
     def landed(tile):
         for j in range(3 * tile, 3 * tile + 3):
@@ -221,17 +235,10 @@
 
     landed(0)
     attend(near, 1, 0)
-    forward(10)
     attend(far, 1, 0)
-    forward(11)
-    turn_w(2)
-    turn_w(3)
-    forward(12)
     landed(1)
     attend(near, 1, 1)
     attend(far, 1, 1)
-    for i in range(4, 8):
-        turn_w(i)
     landed(2)
 
     results = []
@@ -316,7 +323,7 @@
     out[...] = v.astype(BF16)
 
     push.wait_send()
-    for copy in (q_up, q_dn, q_up2, q_dn2):
+    for copy in q_up + q_dn + [q_up2, q_dn2]:
         copy.wait_send()
     for j in range(9):
         y_up_copy(1, j).wait_send()
@@ -343,7 +350,7 @@
         scratch_shapes=[
             pltpu.VMEM((4, 2, width, 128), BF16),
             pltpu.VMEM((32, 64, width), BF16),
-            pltpu.VMEM((2, 36, UNIT, width), BF16),
+            pltpu.VMEM((2, 36, UNIT, 640), BF16),
             pltpu.VMEM((width, 128), BF16),
             pltpu.VMEM((2, LAT, 36 * UNIT), BF16),
             pltpu.VMEM((2, LAT, VH), BF16),
@@ -363,7 +370,7 @@
             pltpu.VMEM((224, 128), F32),
             pltpu.VMEM((3, 224, 128), BF16),
             pltpu.VMEM((3, 224, 128), BF16),
-            dma((5,)), dma((2,)), dma((4,)), dma((4,)),
+            dma((5,)), dma((2,)), dma((6,)), dma((6,)),
             dma((9,)), dma((9,)), dma((9,)), dma((9,)),
             dma((9,)), dma((9,)), dma((9,)), dma((9,)),
             dma((3,)), dma((3,)), dma((3,)), dma((3,)),

time: 85.3 us -> 73.6 us (0.86)
  Pallas kernels: 82.9 us -> 71.3 us
    pallas_call x1, Pallas kernels: 82.9 us -> 71.3 us  [body(): pl.pallas_call(kernel, out_shape=jax.ShapeDtypeStruct((224, 128), BF16),...]
where the time goes in v3:
time: 73.6 us; the launch traced here: 73.4 us
  Pallas kernels  71.3 us (97%)
  local copies, waits for them, and re-layouts  1.45 us (2%)
    pallas_call x1, Pallas kernels, body(): pl.pallas_call(kernel, out_shape=jax.ShapeDtypeStruct((224, 128), BF16),...  71.3 us

profile of v3, /device:TPU:56, one launch (start us, length us, event | category | flops | bytes accessed | tf_op | source)
XLA Modules:
  0.0 73.4 jit_solution(15119137272244914945)
XLA Ops:
  0.7 71.3 %shard_map.73 = bf16[224,128]{1,0:T(8,128)(2,1)} custom-call(s32[16]{0:T(128)} %bitcast.17, s32[1]{0:T(128)S(6)} %copy.9.cached_ref, bf16[2,576,128]{2,1,0:T(8,128)(2,1)} %bitcast.15, bf16[576,128]{1,0:T(8,128)(2,1)} %bitcast.16, bf16[16,64,576]{2,1,0:T(8,128)(2,1)} %bitcast.14, bf16[2,512,128]{2,1,0:T(8,128)(2,1)} %w_uv.1, bf16[256,7168]{1,0:T(8,128)(2,1)} %bitcast.13), custom_call_target="tpu_custom_call" | custom-call | flops 6000000000 | bytes 8000000 | tf_op jit(solution)/shard_map/pallas_call | solution.py:345
  72.0 1.4 %copy.10 = bf16[1,128,224]{1,2,0:T(8,128)(2,1)} copy(bf16[1,128,224]{1,2,0:T(8,128)(2,1)} %bitcast.12) | data formatting | bytes 114688

commit v4 on v3

v4 whole, which is shorter than its diff:
```python
import jax
import jax.numpy as jnp
from jax import lax
from jax.experimental import pallas as pl
from jax.experimental.pallas import tpu as pltpu
from jax.sharding import PartitionSpec as P

MESH = pl.DeviceIdType.MESH
LAT = 512
VH = 128
UNIT = 32
UNITS = 1152 // UNIT
NEW_UNITS = 128 // UNIT
TURNS = UNITS // 4
HOP = 4
TILES = ((0, 384), (384, 896), (896, 1152))
SCALE = 192.0 ** -0.5 * 1.4426950408889634
NEG = -1e30
ZF, YF = 144, 80
Z_ORDER = (4, 3, 5, 2, 6, 1, 7, 0)
Z_GROUPS = ((0, 1), (1, 3), (3, 5), (5, 7), (7, 8))
F32 = jnp.float32
BF16 = jnp.bfloat16


def place():
    c, h, p = lax.axis_index("ctx"), lax.axis_index("head"), lax.axis_index("pool")
    return c // 2, c % 2, h // 4, h % 4, p


def device(x, yh, z, yl, p):
    return {"ctx": x * 2 + yh, "head": z * 4 + yl, "pool": p}


def greet(others):
    barrier = pltpu.get_barrier_semaphore()
    for other in others:
        pl.semaphore_signal(barrier, inc=1, device_id=other, device_id_type=MESH)
    pl.semaphore_wait(barrier, len(others))


def remote(src, dst, send, recv, to):
    return pltpu.make_async_remote_copy(
        src_ref=src, dst_ref=dst, send_sem=send, recv_sem=recv, device_id=to, device_id_type=MESH
    )


def kernel(
    blocks, cached_ref, q_in, new_in, pool_in, w_uv, w_in,
    out,
    qbuf, pbuf0, pbuf1, kbuf, newt, vt, wt, acc, stat, ores, orecv, sstat, srecv,
    w, wo, at, up_out, up_in, dn_out, dn_in, own, y_out, y_in, yf_out, yf_in, zf_out, zf_in,
    lsem, psem, qs, qr, ks, kr, os_, or_, ss, sr,
    us, ur, ds, dr, ys, yr, yfs, yfr, zfs, zfr,
):
    x, yh, z, yl, p = place()
    b = z % 2
    xu, xd, xo = (x + 1) % 4, (x + 3) % 4, (x + 2) % 4
    at_core = device(x, yh, z, yl, 1 - p)
    at_xu, at_xd, at_xo = [device(k, yh, z, yl, p) for k in (xu, xd, xo)]
    y_up, y_dn = (yh * 4 + yl + 1) % 8, (yh * 4 + yl + 7) % 8
    at_yu, at_yd = [device(x, k // 4, z, k % 4, p) for k in (y_up, y_dn)]
    at_z = [device(x, yh, (z + k) % 8, yl, p) for k in range(1, 8)]
    at_zu, at_zd = at_z[0], at_z[6]
    at_y = [device(x, yh, z, (yl + d) % 4, p) for d in (1, 2, 3)]
    cached = cached_ref[0]
    width = q_in.shape[1]
    half = 16

    mine = pl.ds(p * half, half)
    local = [
        pltpu.make_async_copy(pool_in.at[:, pl.ds(0, 32)], pbuf0.at[mine], lsem.at[0]),
        pltpu.make_async_copy(pool_in.at[:, pl.ds(32, 32)], pbuf1.at[mine], lsem.at[5]),
        pltpu.make_async_copy(q_in, qbuf.at[0], lsem.at[1]),
        pltpu.make_async_copy(new_in, newt, lsem.at[2]),
    ]
    load_w = pltpu.make_async_copy(w_in, w, lsem.at[3])
    load_uv = pltpu.make_async_copy(w_uv, wt, lsem.at[4])
    for copy in local + [load_uv, load_w]:
        copy.start()
    greet([at_core, at_xu, at_xd, at_xo, at_yu, at_yd] + at_z + at_y)

    push = []
    for i, pbuf in enumerate((pbuf0, pbuf1)):
        rows = pl.ds(i * 32, 32)
        push.append(remote(pool_in.at[:, rows], pbuf.at[mine], psem.at[i], psem.at[2 + i], at_core))
        push[i].start()
    q_up = [remote(q_in.at[h], qbuf.at[1, h], qs, qr.at[h], at_xu) for h in range(2)]
    q_dn = [remote(q_in.at[h], qbuf.at[2, h], qs, qr.at[2 + h], at_xd) for h in range(2)]
    for copy in (q_up[0], q_dn[1], q_up[1], q_dn[0]):
        copy.start()
    q_up2 = remote(qbuf.at[1, 0], qbuf.at[3, 0], qs, qr.at[4], at_xu)
    q_dn2 = remote(qbuf.at[2, 1], qbuf.at[3, 1], qs, qr.at[5], at_xd)

    for copy in local:
        copy.wait()
    kbuf[0, :, :, width:] = jnp.zeros((UNITS, UNIT, kbuf.shape[-1] - width), BF16)
    kbuf[0, 0:NEW_UNITS, :, :width] = newt[...].T.reshape(NEW_UNITS, UNIT, width)

    def y_up_copy(s, j):
        u = j * 4 + b * 2
        return remote(kbuf.at[s, u], kbuf.at[1, u], ks, kr.at[0, j], at_yu)

    def y_dn_copy(s, j):
        u = j * 4 + b * 2 + 1
        return remote(kbuf.at[s, u], kbuf.at[1, u], ks, kr.at[1, j], at_yd)

    def z_up_copy(j, base):
        u = j * 4 + base * 2
        return remote(kbuf.at[1, u], kbuf.at[1, u], ks, kr.at[2, j], at_zu)

    def z_dn_copy(j, base):
        u = j * 4 + base * 2 + 1
        return remote(kbuf.at[1, u], kbuf.at[1, u], ks, kr.at[3, j], at_zd)

    def first(lo, hi):
        @pl.when(yl == 3)
        def _():
            for j in range(lo, hi):
                y_up_copy(0, j).start()

        @pl.when(yl == 0)
        def _():
            for j in range(lo, hi):
                y_dn_copy(0, j).start()

    first(0, NEW_UNITS // 4)
    per_half = half * 32 // UNIT
    for i, pbuf in enumerate((pbuf0, pbuf1)):
        push[i].wait_recv()

        def gather(k, carry):
            u = NEW_UNITS + i * per_half + k * (32 // UNIT)
            kbuf[0, pl.ds(u, 32 // UNIT), :, :width] = pbuf[blocks[k]].reshape(32 // UNIT, UNIT, width)
            return carry

        lax.fori_loop(0, half, gather, 0)
        first((NEW_UNITS + i * per_half) // 4, (NEW_UNITS + (i + 1) * per_half) // 4)

    def forward(step):
        j = step - HOP * (yl + 1)

        @pl.when((j >= 0) & (j < TURNS))
        def _():
            y_up_copy(1, j).wait_recv()

            @pl.when(yl != 3)
            def _():
                y_up_copy(1, j).start()

            z_up_copy(j, b).start()

        k = step - HOP * (4 - yl)

        @pl.when((k >= 0) & (k < TURNS))
        def _():
            y_dn_copy(1, k).wait_recv()

            @pl.when(yl != 0)
            def _():
                y_dn_copy(1, k).start()

            z_dn_copy(k, b).start()

    owners = [x, xd, xu, xo]

    def attend(slots, s_at, tile):
        c = x * 2 + (yh if s_at == 0 else 1 - yh)
        lo, lanes = slots[0] * 256, len(slots) * 256
        cols = slice(lo, lo + lanes)
        begin, end = TILES[tile]
        rows = end - begin
        keys = kbuf[s_at, begin // UNIT:end // UNIT].reshape(rows, kbuf.shape[-1])[:, :width]
        query = jnp.concatenate([qbuf[g, h] for g in slots for h in range(2)], axis=1)
        s = jnp.dot(keys, query, preferred_element_type=F32) * SCALE
        new = 0 if tile else 128
        row = lax.broadcasted_iota(jnp.int32, (rows - new, lanes), 0) + (begin + new - 128)
        row = ((row >> 5) & 15) * 64 + (row >> 9) * 32 + (row & 31)
        s_hist = jnp.where(row < cached - c * 1024, s[new:], NEG)
        if new:
            token = lax.broadcasted_iota(jnp.int32, (1, 256), 1) % 128
            last = jnp.concatenate([token + (owners[g] * 2 + yh - c) * 128 for g in slots], axis=1)
            row = lax.broadcasted_iota(jnp.int32, (128, lanes), 0)
            s = jnp.concatenate([jnp.where(row <= last, s[:new], NEG), s_hist], axis=0)
        else:
            s = s_hist
        fresh = s_at == 0 and tile == 0
        top = jnp.max(s, axis=0, keepdims=True)
        if not fresh:
            old = stat[0:1, cols]
            top = jnp.maximum(top, old)
        e = jnp.exp2(s - top)
        total = jnp.sum(e, axis=0, keepdims=True)
        o = jnp.dot(vt[s_at, :, begin:end], e.astype(BF16), preferred_element_type=F32)
        if not fresh:
            f = jnp.exp2(old - top)
            total = total + f * stat[1:2, cols]
            o = o + f * acc[:, cols]
        stat[0:1, cols] = top
        stat[1:2, cols] = total
        acc[:, cols] = o

    def turn(s_at, tile):
        begin, end = TILES[tile]
        v = kbuf[s_at, begin // UNIT:end // UNIT].reshape(end - begin, kbuf.shape[-1])[:, :LAT]
        vt[s_at, :, begin:end] = v.T

    def turn_w(i):
        wo[i * 896:(i + 1) * 896] = w[:, i * 896:(i + 1) * 896].T

    near, far = (0, 1), (2, 3)
    for t in range(3):
        turn(0, t)
    q_up[0].wait_recv()
    q_up2.start()
    q_dn[1].wait_recv()
    q_dn2.start()
    load_w.wait()
    load_uv.wait()
    for step in range(HOP, 4 * HOP + TURNS):
        forward(step)
        if step == round(6 * HOP / 4):
            q_up[1].wait_recv()
        if step == round(10 * HOP / 4):
            q_dn[0].wait_recv()
            q_up2.wait_recv()
            q_dn2.wait_recv()
        for t in range(3):
            if step == round((6 + t) * HOP / 4):
                attend(near, 0, t)
            if step == round((10 + t) * HOP / 4):
                attend(far, 0, t)
        for t in range(8):
            if step == round((4 + t if t < 2 else 11 + t) * HOP / 4):
                turn_w(t)

    def landed(tile):
        begin, end = TILES[tile]
        for j in range(begin // UNIT // 4, end // UNIT // 4):
            z_up_copy(j, 1 - b).wait_recv()
            z_dn_copy(j, 1 - b).wait_recv()
        turn(1, tile)

    landed(0)
    attend(near, 1, 0)
    attend(far, 1, 0)
    landed(1)
    attend(near, 1, 1)
    attend(far, 1, 1)
    landed(2)

    results = []
    for slots in (far, near):
        attend(slots, 1, 2)
        for g in reversed(slots):
            cols = slice(g * 256, (g + 1) * 256)
            lat = (acc[:, cols] / stat[1:2, cols]).astype(BF16)
            for h in range(2):
                o = lax.dot_general(
                    wt[h], lat[:, h * 128:(h + 1) * 128], (((0,), (0,)), ((), ())), preferred_element_type=F32
                )
                ores[g, :, h * 128:(h + 1) * 128] = o.astype(BF16)
            if g:
                sstat[g - 1, 0:2] = stat[0:2, cols]
                to = {1: at_xd, 2: at_xu, 3: at_xo}[g]
                sent = [
                    remote(ores.at[g], orecv.at[g - 1], os_, or_.at[g - 1], to),
                    remote(sstat.at[g - 1], srecv.at[g - 1], ss, sr.at[g - 1], to),
                ]
                for copy in sent:
                    copy.start()
                results += sent

    for copy in results:
        copy.wait_recv()
    tops = [stat[0:1, 0:256]] + [srecv[i, 0:1] for i in range(3)]
    sums = [stat[1:2, 0:256]] + [srecv[i, 1:2] for i in range(3)]
    outs = [ores[0]] + [orecv[i] for i in range(3)]
    top = jnp.maximum(jnp.maximum(tops[0], tops[1]), jnp.maximum(tops[2], tops[3]))
    shares = [t * jnp.exp2(m - top) for m, t in zip(tops, sums)]
    inv = 1.0 / (shares[0] + shares[1] + shares[2] + shares[3])
    head = sum(o.astype(F32) * (s * inv) for o, s in zip(outs, shares))
    for h in range(2):
        at[h * 128:(h + 1) * 128] = head[:, h * 128:(h + 1) * 128].astype(BF16)

    a = at[...]

    def term(dest, d, lo, rows):
        row = pl.multiple_of((dest % 8) * 896 + ((yl + 1 + d) % 4) * 224 + lo, 16)
        return jnp.dot(wo[pl.ds(row, rows)], a, preferred_element_type=F32)

    def slot(s, d):
        return s * 4 - 2 + d if s else d % 2

    def flow(way, s, d):
        i = slot(s, d)
        if way == "up":
            return remote(up_out.at[i], up_in.at[i], us, ur.at[i], at_zu)
        return remote(dn_out.at[i], dn_in.at[i], ds, dr.at[i], at_zd)

    def ring(s, order):
        for way, d in order:
            sent, got = (up_out, up_in) if way == "up" else (dn_out, dn_in)
            v = term(z + 4 - s if way == "up" else z + 4 + s, d, 0, ZF)
            if s > 1 or (s == 1 and (d >= 2) == (way == "up")):
                flow(way, s - 1, d).wait_recv()
                v = v + got[slot(s - 1, d)].astype(F32)
            sent[slot(s, d)] = v.astype(BF16)
            flow(way, s, d).start()

    def y_first(g, d):
        lo, hi = Z_GROUPS[g]
        rows = pl.ds(lo, hi - lo)
        return remote(yf_out.at[d, rows], yf_in.at[d, rows], yfs, yfr.at[d, g], at_y[d])

    def send_group(g):
        for d in range(3):
            for i in range(*Z_GROUPS[g]):
                yf_out[d, i] = term(z + Z_ORDER[i], d, ZF, YF).astype(BF16)
            y_first(g, d).start()

    def z_last(i):
        to = device(x, yh, (z + Z_ORDER[i]) % 8, yl, p)
        return remote(zf_out.at[i], zf_in.at[i], zfs, zfr.at[i], to)

    def take_group(g):
        for d in range(3):
            y_first(g, d).wait_recv()
        for i in range(*Z_GROUPS[g]):
            v = term(z + Z_ORDER[i], 3, ZF, YF)
            for d in range(3):
                v = v + yf_in[d, i].astype(F32)
            if Z_ORDER[i]:
                zf_out[i] = v.astype(BF16)
                z_last(i).start()
            else:
                own[ZF:] = v

    def y_last(d):
        return remote(y_out.at[d], y_in.at[d], ys, yr.at[d], at_y[d])

    ring(0, (("up", 2), ("dn", 0), ("up", 3), ("dn", 1)))
    send_group(0)
    ring(1, (("up", 0), ("dn", 2), ("up", 1), ("dn", 3)))
    send_group(1)
    ring(1, (("dn", 0), ("up", 2), ("dn", 1), ("up", 3)))
    send_group(2)
    send_group(3)
    ring(2, (("up", 0), ("dn", 2), ("up", 1), ("dn", 3)))
    take_group(0)
    send_group(4)
    ring(2, (("up", 2), ("dn", 0), ("up", 3), ("dn", 1)))
    take_group(1)
    ring(3, (("up", 0), ("dn", 2), ("up", 1), ("dn", 0)))
    take_group(2)
    ring(3, (("up", 2), ("dn", 1), ("up", 3), ("dn", 3)))
    take_group(3)
    for d in (0, 2, 1, 3):
        v = term(z, d, 0, ZF)
        flow("up", 3, d).wait_recv()
        flow("dn", 3, d).wait_recv()
        i = slot(3, d)
        v = v + up_in[i].astype(F32) + dn_in[i].astype(F32)
        if d < 3:
            y_out[d] = v.astype(BF16)
            y_last(d).start()
        else:
            own[:ZF] = v
    take_group(4)
    v = own[ZF:]
    for i in range(7):
        z_last(i).wait_recv()
        v = v + zf_in[i].astype(F32)
    out[ZF:] = v.astype(BF16)
    v = own[:ZF]
    for d in range(3):
        y_last(d).wait_recv()
        v = v + y_in[d].astype(F32)
    out[:ZF] = v.astype(BF16)

    for copy in push:
        copy.wait_send()
    for ref, sem in (
        (qbuf.at[pl.ds(0, 3)], qs), (kbuf.at[1], ks), (orecv, os_), (srecv, ss), (up_out, us), (dn_out, ds),
        (yf_out, yfs), (zf_out, zfs), (y_out, ys),
    ):
        pltpu.make_async_copy(ref, ref, sem).wait()


def body(queries, new_latent, cache_pool, block_list, cached_lengths, w_uv, w_o):
    width = queries.shape[-1]
    columns = w_o.shape[-1]
    q = jnp.transpose(queries[0], (1, 2, 0))
    new = new_latent[0].T
    hbm = pl.BlockSpec(memory_space=pltpu.HBM)
    smem = pl.BlockSpec(memory_space=pltpu.SMEM)
    dma = pltpu.SemaphoreType.DMA
    mixed = pl.pallas_call(
        kernel,
        out_shape=jax.ShapeDtypeStruct((224, 128), BF16),
        in_specs=[smem, smem, hbm, hbm, hbm, hbm, hbm],
        out_specs=pl.BlockSpec(memory_space=pltpu.VMEM),
        scratch_shapes=[
            pltpu.VMEM((4, 2, width, 128), BF16),
            pltpu.VMEM((32, 32, width), BF16),
            pltpu.VMEM((32, 32, width), BF16),
            pltpu.VMEM((2, UNITS, UNIT, 640), BF16),
            pltpu.VMEM((width, 128), BF16),
            pltpu.VMEM((2, LAT, 1152), BF16),
            pltpu.VMEM((2, LAT, VH), BF16),
            pltpu.VMEM((LAT, 1024), F32),
            pltpu.VMEM((8, 1024), F32),
            pltpu.VMEM((4, VH, 256), BF16),
            pltpu.VMEM((3, VH, 256), BF16),
            pltpu.VMEM((3, 8, 256), F32),
            pltpu.VMEM((3, 8, 256), F32),
            pltpu.VMEM((256, columns), BF16),
            pltpu.VMEM((columns, 256), BF16),
            pltpu.VMEM((256, 128), BF16),
            pltpu.VMEM((14, ZF, 128), BF16),
            pltpu.VMEM((14, ZF, 128), BF16),
            pltpu.VMEM((14, ZF, 128), BF16),
            pltpu.VMEM((14, ZF, 128), BF16),
            pltpu.VMEM((224, 128), F32),
            pltpu.VMEM((3, ZF, 128), BF16),
            pltpu.VMEM((3, ZF, 128), BF16),
            pltpu.VMEM((3, 8, YF, 128), BF16),
            pltpu.VMEM((3, 8, YF, 128), BF16),
            pltpu.VMEM((7, YF, 128), BF16),
            pltpu.VMEM((7, YF, 128), BF16),
            dma((6,)), dma((4,)), dma, dma((6,)), dma, dma((4, TURNS)), dma, dma((3,)), dma, dma((3,)),
            dma, dma((14,)), dma, dma((14,)), dma, dma((3,)), dma, dma((3, 5)), dma, dma((7,)),
        ],
        compiler_params=pltpu.CompilerParams(
            collective_id=0, has_side_effects=True, vmem_limit_bytes=56 * 2**20
        ),
        cost_estimate=pl.CostEstimate(flops=6 * 10**9, bytes_accessed=8 * 10**6, transcendentals=2 * 10**6),
    )(block_list[0, 0], cached_lengths, q, new, cache_pool[0], w_uv, w_o.reshape(256, columns))
    return mixed.T[None]


def solution(mesh):
    in_specs = (
        P("pool", "ctx", "head", None),
        P("pool", "ctx", None),
        P("ctx", "pool", None, None),
        P("pool", "ctx", None),
        P("pool"),
        P("head", None, None),
        P("head", None, None),
    )
    out_specs = P("pool", "ctx", "head")
    return jax.shard_map(body, mesh=mesh, in_specs=in_specs, out_specs=out_specs, check_vma=False)
```

time: 73.6 us -> 72 us (0.978); the launches traced: 73.4 us -> 70.7 us
  Pallas kernels: 71.3 us -> 68.6 us
    pallas_call x1, Pallas kernels: 71.3 us -> 68.6 us  [body(): pl.pallas_call(kernel, out_shape=jax.ShapeDtypeStruct((224, 128), BF16),...]
where the time goes in v4:
time: 72 us; the launch traced here: 70.7 us
  Pallas kernels  68.6 us (95%)
  local copies, waits for them, and re-layouts  1.45 us (2%)
    pallas_call x1, Pallas kernels, body(): pl.pallas_call(kernel, out_shape=jax.ShapeDtypeStruct((224, 128), BF16),...  68.6 us
    unnamed x1, local copies, waits for them, and re-layouts  1.45 us

profile of v4, /device:TPU:56, one launch (start us, length us, event | category | flops | bytes accessed | tf_op | source)
XLA Modules:
  0.0 70.7 jit_solution(6978085011688100452)
XLA Ops:
  0.7 68.6 %shard_map.73 = bf16[224,128]{1,0:T(8,128)(2,1)} custom-call(s32[16]{0:T(128)} %bitcast.17, s32[1]{0:T(128)S(6)} %copy.9.cached_ref, bf16[2,576,128]{2,1,0:T(8,128)(2,1)} %bitcast.15, bf16[576,128]{1,0:T(8,128)(2,1)} %bitcast.16, bf16[16,64,576]{2,1,0:T(8,128)(2,1)} %bitcast.14, bf16[2,512,128]{2,1,0:T(8,128)(2,1)} %w_uv.1, bf16[256,7168]{1,0:T(8,128)(2,1)} %bitcast.13), custom_call_target="tpu_custom_call" | custom-call | flops 6000000000 | bytes 8000000 | tf_op jit(solution)/shard_map/pallas_call | solution.py:398
  69.3 1.4 %copy.10 = bf16[1,128,224]{1,2,0:T(8,128)(2,1)} copy(bf16[1,128,224]{1,2,0:T(8,128)(2,1)} %bitcast.12) | data formatting | bytes 114688

commit v5 on v4

--- a/solution.py
+++ b/solution.py
@@ -241,35 +241,29 @@
             z_dn_copy(j, 1 - b).wait_recv()
         turn(1, tile)
 
-    landed(0)
-    attend(near, 1, 0)
-    attend(far, 1, 0)
-    landed(1)
-    attend(near, 1, 1)
-    attend(far, 1, 1)
-    landed(2)
+    for tile in range(3):
+        landed(tile)
+        attend(near + far, 1, tile)
 
     results = []
-    for slots in (far, near):
-        attend(slots, 1, 2)
-        for g in reversed(slots):
-            cols = slice(g * 256, (g + 1) * 256)
-            lat = (acc[:, cols] / stat[1:2, cols]).astype(BF16)
-            for h in range(2):
-                o = lax.dot_general(
-                    wt[h], lat[:, h * 128:(h + 1) * 128], (((0,), (0,)), ((), ())), preferred_element_type=F32
-                )
-                ores[g, :, h * 128:(h + 1) * 128] = o.astype(BF16)
-            if g:
-                sstat[g - 1, 0:2] = stat[0:2, cols]
-                to = {1: at_xd, 2: at_xu, 3: at_xo}[g]
-                sent = [
-                    remote(ores.at[g], orecv.at[g - 1], os_, or_.at[g - 1], to),
-                    remote(sstat.at[g - 1], srecv.at[g - 1], ss, sr.at[g - 1], to),
-                ]
-                for copy in sent:
-                    copy.start()
-                results += sent
+    for g in (3, 1, 2, 0):
+        cols = slice(g * 256, (g + 1) * 256)
+        lat = (acc[:, cols] * (1.0 / stat[1:2, cols])).astype(BF16)
+        for h in range(2):
+            o = lax.dot_general(
+                wt[h], lat[:, h * 128:(h + 1) * 128], (((0,), (0,)), ((), ())), preferred_element_type=F32
+            )
+            ores[g, :, h * 128:(h + 1) * 128] = o.astype(BF16)
+        if g:
+            sstat[g - 1, 0:2] = stat[0:2, cols]
+            to = {1: at_xd, 2: at_xu, 3: at_xo}[g]
+            sent = [
+                remote(ores.at[g], orecv.at[g - 1], os_, or_.at[g - 1], to),
+                remote(sstat.at[g - 1], srecv.at[g - 1], ss, sr.at[g - 1], to),
+            ]
+            for copy in sent:
+                copy.start()
+            results += sent
 
     for copy in results:
         copy.wait_recv()
@@ -299,9 +293,9 @@
         return remote(dn_out.at[i], dn_in.at[i], ds, dr.at[i], at_zd)
 
     def ring(s, order):
-        for way, d in order:
+        own_terms = [term(z + 4 - s if way == "up" else z + 4 + s, d, 0, ZF) for way, d in order]
+        for (way, d), v in zip(order, own_terms):
             sent, got = (up_out, up_in) if way == "up" else (dn_out, dn_in)
-            v = term(z + 4 - s if way == "up" else z + 4 + s, d, 0, ZF)
             if s > 1 or (s == 1 and (d >= 2) == (way == "up")):
                 flow(way, s - 1, d).wait_recv()
                 v = v + got[slot(s - 1, d)].astype(F32)
@@ -324,10 +318,11 @@
         return remote(zf_out.at[i], zf_in.at[i], zfs, zfr.at[i], to)
 
     def take_group(g):
+        members = range(*Z_GROUPS[g])
+        own_terms = [term(z + Z_ORDER[i], 3, ZF, YF) for i in members]
         for d in range(3):
             y_first(g, d).wait_recv()
-        for i in range(*Z_GROUPS[g]):
-            v = term(z + Z_ORDER[i], 3, ZF, YF)
+        for i, v in zip(members, own_terms):
             for d in range(3):
                 v = v + yf_in[d, i].astype(F32)
             if Z_ORDER[i]:
@@ -355,8 +350,9 @@
     take_group(2)
     ring(3, (("up", 2), ("dn", 1), ("up", 3), ("dn", 3)))
     take_group(3)
-    for d in (0, 2, 1, 3):
-        v = term(z, d, 0, ZF)
+    order = (0, 2, 1, 3)
+    own_terms = [term(z, d, 0, ZF) for d in order]
+    for d, v in zip(order, own_terms):
         flow("up", 3, d).wait_recv()
         flow("dn", 3, d).wait_recv()
         i = slot(3, d)

time: 72 us -> 71.8 us (level)
  no operation moved by 1% of the time
where the time goes in v5:
time: 71.8 us; the launch traced here: 70.5 us
  Pallas kernels  68.4 us (95%)
  local copies, waits for them, and re-layouts  1.45 us (2%)
    pallas_call x1, Pallas kernels, body(): pl.pallas_call(kernel, out_shape=jax.ShapeDtypeStruct((224, 128), BF16),...  68.4 us
    unnamed x1, local copies, waits for them, and re-layouts  1.45 us

profile of v5, /device:TPU:56, one launch (start us, length us, event | category | flops | bytes accessed | tf_op | source)
XLA Modules:
  0.0 70.5 jit_solution(357979463691942015)
XLA Ops:
  0.7 68.4 %shard_map.73 = bf16[224,128]{1,0:T(8,128)(2,1)} custom-call(s32[16]{0:T(128)} %bitcast.17, s32[1]{0:T(128)S(6)} %copy.9.cached_ref, bf16[2,576,128]{2,1,0:T(8,128)(2,1)} %bitcast.15, bf16[576,128]{1,0:T(8,128)(2,1)} %bitcast.16, bf16[16,64,576]{2,1,0:T(8,128)(2,1)} %bitcast.14, bf16[2,512,128]{2,1,0:T(8,128)(2,1)} %w_uv.1, bf16[256,7168]{1,0:T(8,128)(2,1)} %bitcast.13), custom_call_target="tpu_custom_call" | custom-call | flops 6000000000 | bytes 8000000 | tf_op jit(solution)/shard_map/pallas_call | solution.py:394
  69.1 1.4 %copy.10 = bf16[1,128,224]{1,2,0:T(8,128)(2,1)} copy(bf16[1,128,224]{1,2,0:T(8,128)(2,1)} %bitcast.12) | data formatting | bytes 114688

commit v6 on v5

--- a/solution.py
+++ b/solution.py
@@ -231,7 +231,7 @@
             if step == round((10 + t) * HOP / 4):
                 attend(far, 0, t)
         for t in range(8):
-            if step == round((4 + t if t < 2 else 11 + t) * HOP / 4):
+            if step == round((4 + t // 2) * HOP / 4):
                 turn_w(t)
 
     def landed(tile):

time: 71.8 us -> 71.8 us (level)
  no operation moved by 1% of the time
where the time goes in v6:
time: 71.8 us; the launch traced here: 70.5 us
  Pallas kernels  68.4 us (95%)
  local copies, waits for them, and re-layouts  1.45 us (2%)
    pallas_call x1, Pallas kernels, body(): pl.pallas_call(kernel, out_shape=jax.ShapeDtypeStruct((224, 128), BF16),...  68.4 us
    unnamed x1, local copies, waits for them, and re-layouts  1.45 us

profile of v6, /device:TPU:56, one launch (start us, length us, event | category | flops | bytes accessed | tf_op | source)
XLA Modules:
  0.0 70.5 jit_solution(7101853240139019663)
XLA Ops:
  0.7 68.4 %shard_map.73 = bf16[224,128]{1,0:T(8,128)(2,1)} custom-call(s32[16]{0:T(128)} %bitcast.17, s32[1]{0:T(128)S(6)} %copy.9.cached_ref, bf16[2,576,128]{2,1,0:T(8,128)(2,1)} %bitcast.15, bf16[576,128]{1,0:T(8,128)(2,1)} %bitcast.16, bf16[16,64,576]{2,1,0:T(8,128)(2,1)} %bitcast.14, bf16[2,512,128]{2,1,0:T(8,128)(2,1)} %w_uv.1, bf16[256,7168]{1,0:T(8,128)(2,1)} %bitcast.13), custom_call_target="tpu_custom_call" | custom-call | flops 6000000000 | bytes 8000000 | tf_op jit(solution)/shard_map/pallas_call | solution.py:394
  69.1 1.4 %copy.10 = bf16[1,128,224]{1,2,0:T(8,128)(2,1)} copy(bf16[1,128,224]{1,2,0:T(8,128)(2,1)} %bitcast.12) | data formatting | bytes 114688
